TPU v7x, 128 devices: a whole 4x4x4 slice. The times are simulated.
128 devices in a mesh: lat: 4 (over y_hi, core), lon: 32 (over y_lo, x, z).
Axes of the slice: x: 4, y: 4 (y_hi: 2, y_lo: 2; y = y_hi * 2 + y_lo), z: 4, core: 2. Of those that a mesh axis runs over, the one named last changes fastest.
Arguments:
- latent_field: bfloat16 [2, 192, 1152, 512], P(None, 'lat', 'lon'), may hold values from -6 to 6
- land_mask: int32 [192, 1152], P('lat', 'lon'), may hold values 0 or 1
- padded: int32 [192, 1152], P('lat', 'lon'), may hold values 0 or 1
- norm1_gain: float32 [512], replicated, may hold values from 0.1 to 1.9
- qkv_weight: bfloat16 [512, 1536], replicated, may hold values from -0.25 to 0.25
- land_bias: float32 [16], replicated, may hold values from -2 to 300
- out_weight: bfloat16 [512, 512], replicated, may hold values from -0.25 to 0.25
- norm2_gain: float32 [512], replicated, may hold values from 0.1 to 1.9
- up_weight: bfloat16 [512, 2048], replicated, may hold values from -0.25 to 0.25
- down_weight: bfloat16 [2048, 512], replicated, may hold values from -0.125 to 0.125
Outputs:
- mixed: bfloat16 [2, 192, 1152, 512], P(None, 'lat', 'lon')
Inputs may be any that keep to these rules, and one draw needn't show every extreme that they name: `land_mask`: 1 marks land. `padded`: 1 marks a padding cell.
All inputs are finite; a program needn't handle non-finite values. No bound on the sum of `land_mask` or of `padded` on one device may be relied on, other than what follows from the above.
Results may differ from a plain program's by a relative error of at most 0.007.
Values may be sent and summed in bfloat16 or wider, within the bound.
No kernel may reach another device: no remote copies, remote signals or barrier semaphores. Data moves between devices by JAX's collectives and lax.ppermute only.
A program may use at most 192 MiB of HBM per device.

v0:
```python
import math

import jax
import jax.numpy as jnp
from jax import lax
from jax.sharding import PartitionSpec as P

WIN = 12
SHIFT = 6


def from_behind(value, axis, by):
    devices = lax.axis_size(axis)
    return lax.ppermute(value, axis, [(i, (i + by) % devices) for i in range(devices)])


def layer_norm(values_in, gain):
    wide = values_in.astype(jnp.float32)
    center = wide - jnp.mean(wide, axis=-1, keepdims=True)
    spread = jnp.mean(center * center, axis=-1, keepdims=True)
    return (center * lax.rsqrt(spread + 1e-05) * gain).astype(jnp.bfloat16)


def attend_windows(
    tokens, land_tok, pad_tok, polar_tok, norm1_gain, qkv_weight, land_bias, out_weight
):
    windows_n, count, channels = tokens.shape
    heads = land_bias.shape[0]
    head_size = channels // heads
    normed = layer_norm(tokens, norm1_gain)
    packed = jnp.einsum(
        "wnd,de->wne", normed, qkv_weight, preferred_element_type=jnp.float32
    ).astype(jnp.bfloat16)
    packed = packed.reshape(windows_n, count, 3, heads, head_size)
    queries = packed[:, :, 0]
    key_rows = packed[:, :, 1]
    val_rows = packed[:, :, 2]
    scores = jnp.einsum(
        "wqhe,wkhe->whqk", queries, key_rows, preferred_element_type=jnp.float32
    ) * (1.0 / math.sqrt(head_size))
    land_f = land_tok.astype(jnp.float32)
    scores = (
        scores + land_bias[None, :, None, None] * (land_f[:, :, None] * land_f[:, None, :])[:, None]
    )
    same_group = polar_tok[:, :, None] == polar_tok[:, None, :]
    itself = jnp.eye(count, dtype=jnp.bool_)
    allowed = same_group & ((pad_tok[:, None, :] == 0) | itself[None])
    scores = jnp.where(allowed[:, None], scores, -1e30)
    row_max = jnp.max(scores, axis=-1, keepdims=True)
    raised = jnp.exp(scores - row_max)
    attn_weights = (raised / jnp.sum(raised, axis=-1, keepdims=True)).astype(jnp.bfloat16)
    heads_out = jnp.einsum(
        "whqk,wkhe->wqhe", attn_weights, val_rows, preferred_element_type=jnp.float32
    ).astype(jnp.bfloat16)
    heads_out = heads_out.reshape(windows_n, count, channels)
    return jnp.einsum(
        "wnd,de->wne", heads_out, out_weight, preferred_element_type=jnp.float32
    ).astype(jnp.bfloat16)


def window_attention(block, masks, polar, norm1_gain, qkv_weight, land_bias, out_weight):
    levels, height, breadth, channels = block.shape
    band_n = height // WIN
    col_n = breadth // WIN
    count = levels * WIN * WIN
    tiles = (
        block.reshape(levels, band_n, WIN, col_n, WIN, channels)
        .transpose(1, 3, 0, 2, 4, 5)
        .reshape(band_n, col_n, count, channels)
    )

    def spread_cells(cells):
        arranged = cells.reshape(band_n, WIN, col_n, WIN).transpose(0, 2, 1, 3)[:, :, None]
        return jnp.broadcast_to(arranged, (band_n, col_n, levels, WIN, WIN)).reshape(
            band_n, col_n, count
        )

    land_tok = spread_cells(masks[0])
    pad_tok = spread_cells(masks[1])
    polar_tok = spread_cells(jnp.broadcast_to(polar[:, None], (height, breadth)))

    def one_band(parts):
        return attend_windows(
            parts[0], parts[1], parts[2], parts[3], norm1_gain, qkv_weight, land_bias, out_weight
        )

    outcome = lax.map(one_band, (tiles, land_tok, pad_tok, polar_tok))
    return (
        outcome.reshape(band_n, col_n, levels, WIN, WIN, channels)
        .transpose(2, 0, 3, 1, 4, 5)
        .reshape(levels, height, breadth, channels)
    )


def feed_forward(latent_field, attended, norm2_gain, up_weight, down_weight):
    residual = latent_field.astype(jnp.float32) + attended.astype(jnp.float32)
    normed = layer_norm(residual, norm2_gain).reshape(-1, residual.shape[-1])
    hidden = jax.nn.gelu(
        jnp.dot(normed, up_weight, preferred_element_type=jnp.float32), approximate=False
    ).astype(jnp.bfloat16)
    output = residual + jnp.dot(hidden, down_weight, preferred_element_type=jnp.float32).reshape(
        residual.shape
    )
    return output.astype(jnp.bfloat16)


def on_device(
    latent_field,
    land_mask,
    padded,
    norm1_gain,
    qkv_weight,
    land_bias,
    out_weight,
    norm2_gain,
    up_weight,
    down_weight,
):
    levels, height, breadth, channels = latent_field.shape
    masks = jnp.stack([land_mask, padded])
    lat_position = lax.axis_index("lat")
    lat_total = height * lax.axis_size("lat")
    strip, strip_masks = from_behind((latent_field[:, :SHIFT], masks[:, :SHIFT]), "lat", -1)
    tall = jnp.concatenate([latent_field[:, SHIFT:], strip], 1)
    tall_masks = jnp.concatenate([masks[:, SHIFT:], strip_masks], 1)
    side, side_masks = from_behind((tall[:, :, :SHIFT], tall_masks[:, :, :SHIFT]), "lon", -1)
    block = jnp.concatenate([tall[:, :, SHIFT:], side], 2)
    block_masks = jnp.concatenate([tall_masks[:, :, SHIFT:], side_masks], 2)
    start_row = lat_position * height + SHIFT
    polar = ((start_row + jnp.arange(height, dtype=jnp.int32)) % lat_total < SHIFT).astype(
        jnp.int32
    )
    moved = window_attention(
        block, block_masks, polar, norm1_gain, qkv_weight, land_bias, out_weight
    )
    back_rows = from_behind(moved[:, height - SHIFT :], "lat", 1)
    upright = jnp.concatenate([back_rows, moved[:, : height - SHIFT]], 1)
    back_cols = from_behind(upright[:, :, breadth - SHIFT :], "lon", 1)
    attended = jnp.concatenate([back_cols, upright[:, :, : breadth - SHIFT]], 2)
    return feed_forward(latent_field, attended, norm2_gain, up_weight, down_weight)


def solution(mesh):
    placed = (
        P(None, "lat", "lon", None),
        P("lat", "lon"),
        P("lat", "lon"),
        P(),
        P(),
        P(),
        P(),
        P(),
        P(),
        P(),
    )
    return jax.shard_map(
        on_device,
        mesh=mesh,
        in_specs=placed,
        out_specs=P(None, "lat", "lon", None),
        check_vma=False,
    )
```

profile of v0, /device:TPU:1, one launch (start us, length us, event | category | flops | bytes accessed | tf_op | source)
XLA Modules:
  0.0 368.2 jit_solution(1137064904062559740)
XLA Ops:
  7.0 5.9 %slice.51 = bf16[2,42,36,512]{3,1,2,0:T(8,128)(2,1)} slice(bf16[2,48,36,512]{3,1,2,0:T(8,128)(2,1)} %param.12), slice={[0:2], [6:48], [0:36], [0:512]} | slice | bytes 6193152 | tf_op jit(solution)/shard_map/slice | solution.py:124
  15.1 6.1 %collective-permute-start.1 = (bf16[2,48,6,512]{3,1,2,0:T(8,128)(2,1)}, bf16[2,48,6,512]{3,1,2,0:T(8,128)(2,1)S(1)}, u32[]{:S(2)}, u32[]{:S(2)}) collective-permute-start(bf16[2,48,6,512]{3,1,2,0:T(8,128)(2,1)} %pad_maximum_fusion.3), channel_id=1, source_target_pairs={{0,31},{1,0},{2,1},{3,2},{4,3},{5,4},{6,5},{7,6},{8,7},{9,8},{10,9... | collective-permute-start | bytes 1769480 | tf_op jit(solution)/shard_map/ppermute | solution.py:14
  22.4 11.1 %collective-permute-done.3 = s32[2,48,6]{1,2,0:T(8,128)S(1)} collective-permute-done((s32[2,48,6]{1,2,0:T(8,128)S(1)}, s32[2,48,6]{1,2,0:T(8,128)S(1)}, u32[]{:S(2)}, u32[]{:S(2)}) %collective-permute-start.3) | collective-permute-done | bytes 2336 | tf_op jit(solution)/shard_map/ppermute | solution.py:14
  40.0 3.6 copy.90
  49.0 168.3 %while.10 = (s32[]{:T(128)}, bf16[4,3,288,512]{3,2,1,0:T(8,128)(2,1)}, bf16[4,3,288,512]{3,2,1,0:T(8,128)(2,1)}, f32[512]{0:T(512)S(1)}, bf16[512,1536]{1,0:T(8,...) while((s32[]{:T(128)}, ...), condition=%wide.region_5.6_spmd, body=%wide.region_0.5_spmd.sunk | while | flops 2636281344 | bytes 24841676 | solution.py:87
  53.8 4.9 %convolution_convert_fusion.3 = bf16[3,288,1536]{2,1,0:T(8,128)(2,1)} fusion(bf16[512,1536]{1,0:T(8,128)(2,1)} %get-tuple-element.213, f32[512]{0:T(512)S(1)} %get-tuple-element.212, f32[3,288]{1,0:T(4,128)S(1)} %add_rsqrt_fusion.3, f32[3,288]{1,0:T(4,128)S(1)} %broadcast_multiply_fusion.6, bf16[4,3,288,512]{3,2,1,0:T(8,128)(2,1)} %get-tuple-element.211, ...), kind=kOutput, calls=%fused_computation.11.clone.1 | convolution fusion | flops 1362493440 | bytes 5120772 | tf_op jit(solution)/shard_map/while/body/eval_jaxpr/wnd,de->wne/dot_general | solution.py:31
  58.7 4.7 %copy.126 = bf16[3,288,1536]{1,2,0:T(8,128)(2,1)} copy(bf16[3,288,1536]{2,1,0:T(8,128)(2,1)} %convolution_convert_fusion.3) | data formatting | bytes 5308416 | tf_op jit(solution)/shard_map/while/body/eval_jaxpr/convert_element_type | solution.py:33
  63.3 11.7 %fusion.125 = f32[3,16,288]{2,1,0:T(8,128)} fusion(f32[3,288,288]{1,2,0:T(8,128)S(1)} %broadcast_multiply_fusion.5, f32[16]{0:T(128)S(1)} %get-tuple-element.216, pred[3,288,288]{1,2,0:T(8,128)(4,1)} %or_and_fusion.2, bf16[3,288,3,16,32]{1,4,3,2,0:T(8,128)(2,1)} %bitcast.132), kind=kOutput, calls=%fused_computation.137.clone.1 | convolution fusion | flops 278692128 | bytes 3741760 | tf_op jit(solution)/shard_map/while/body/eval_jaxpr/sub | solution.py:50
  75.1 13.3 %fusion.126 = bf16[3,16,32,288]{3,2,1,0:T(8,128)(2,1)} fusion(f32[3,16,288]{2,1,0:T(8,128)} %fusion.125, bf16[3,288,3,16,32]{1,4,3,2,0:T(8,128)(2,1)} %bitcast.133, f32[3,288,288]{1,2,0:T(8,128)S(1)} %broadcast_multiply_fusion.5, f32[16]{0:T(128)S(1)} %get-tuple-element.216, pred[3,288,288]{1,2,0:T(8,128)(4,1)} %or_and_fusion.2), kind=kOutput, calls=%fused_computation.22.clone.1 | convolution fusion | flops 537933568 | bytes 4838464 | tf_op jit(solution)/shard_map/while/body/eval_jaxpr/whqk,wkhe->wqhe/dot_general | solution.py:52
  95.7 4.9 %convolution_convert_fusion.3 = bf16[3,288,1536]{2,1,0:T(8,128)(2,1)} fusion(bf16[512,1536]{1,0:T(8,128)(2,1)} %get-tuple-element.213, f32[512]{0:T(512)S(1)} %get-tuple-element.212, f32[3,288]{1,0:T(4,128)S(1)} %add_rsqrt_fusion.3, f32[3,288]{1,0:T(4,128)S(1)} %broadcast_multiply_fusion.6, bf16[4,3,288,512]{3,2,1,0:T(8,128)(2,1)} %get-tuple-element.211, ...), kind=kOutput, calls=%fused_computation.11.clone.1 | convolution fusion | flops 1362493440 | bytes 5120772 | tf_op jit(solution)/shard_map/while/body/eval_jaxpr/wnd,de->wne/dot_general | solution.py:31
  100.6 4.7 %copy.126 = bf16[3,288,1536]{1,2,0:T(8,128)(2,1)} copy(bf16[3,288,1536]{2,1,0:T(8,128)(2,1)} %convolution_convert_fusion.3) | data formatting | bytes 5308416 | tf_op jit(solution)/shard_map/while/body/eval_jaxpr/convert_element_type | solution.py:33
  105.3 11.7 %fusion.125 = f32[3,16,288]{2,1,0:T(8,128)} fusion(f32[3,288,288]{1,2,0:T(8,128)S(1)} %broadcast_multiply_fusion.5, f32[16]{0:T(128)S(1)} %get-tuple-element.216, pred[3,288,288]{1,2,0:T(8,128)(4,1)} %or_and_fusion.2, bf16[3,288,3,16,32]{1,4,3,2,0:T(8,128)(2,1)} %bitcast.132), kind=kOutput, calls=%fused_computation.137.clone.1 | convolution fusion | flops 278692128 | bytes 3741760 | tf_op jit(solution)/shard_map/while/body/eval_jaxpr/sub | solution.py:50
  117.0 13.3 %fusion.126 = bf16[3,16,32,288]{3,2,1,0:T(8,128)(2,1)} fusion(f32[3,16,288]{2,1,0:T(8,128)} %fusion.125, bf16[3,288,3,16,32]{1,4,3,2,0:T(8,128)(2,1)} %bitcast.133, f32[3,288,288]{1,2,0:T(8,128)S(1)} %broadcast_multiply_fusion.5, f32[16]{0:T(128)S(1)} %get-tuple-element.216, pred[3,288,288]{1,2,0:T(8,128)(4,1)} %or_and_fusion.2), kind=kOutput, calls=%fused_computation.22.clone.1 | convolution fusion | flops 537933568 | bytes 4838464 | tf_op jit(solution)/shard_map/while/body/eval_jaxpr/whqk,wkhe->wqhe/dot_general | solution.py:52
  137.7 4.9 %convolution_convert_fusion.3 = bf16[3,288,1536]{2,1,0:T(8,128)(2,1)} fusion(bf16[512,1536]{1,0:T(8,128)(2,1)} %get-tuple-element.213, f32[512]{0:T(512)S(1)} %get-tuple-element.212, f32[3,288]{1,0:T(4,128)S(1)} %add_rsqrt_fusion.3, f32[3,288]{1,0:T(4,128)S(1)} %broadcast_multiply_fusion.6, bf16[4,3,288,512]{3,2,1,0:T(8,128)(2,1)} %get-tuple-element.211, ...), kind=kOutput, calls=%fused_computation.11.clone.1 | convolution fusion | flops 1362493440 | bytes 5120772 | tf_op jit(solution)/shard_map/while/body/eval_jaxpr/wnd,de->wne/dot_general | solution.py:31
  142.5 4.7 %copy.126 = bf16[3,288,1536]{1,2,0:T(8,128)(2,1)} copy(bf16[3,288,1536]{2,1,0:T(8,128)(2,1)} %convolution_convert_fusion.3) | data formatting | bytes 5308416 | tf_op jit(solution)/shard_map/while/body/eval_jaxpr/convert_element_type | solution.py:33
  147.2 11.7 %fusion.125 = f32[3,16,288]{2,1,0:T(8,128)} fusion(f32[3,288,288]{1,2,0:T(8,128)S(1)} %broadcast_multiply_fusion.5, f32[16]{0:T(128)S(1)} %get-tuple-element.216, pred[3,288,288]{1,2,0:T(8,128)(4,1)} %or_and_fusion.2, bf16[3,288,3,16,32]{1,4,3,2,0:T(8,128)(2,1)} %bitcast.132), kind=kOutput, calls=%fused_computation.137.clone.1 | convolution fusion | flops 278692128 | bytes 3741760 | tf_op jit(solution)/shard_map/while/body/eval_jaxpr/sub | solution.py:50
  158.9 13.3 %fusion.126 = bf16[3,16,32,288]{3,2,1,0:T(8,128)(2,1)} fusion(f32[3,16,288]{2,1,0:T(8,128)} %fusion.125, bf16[3,288,3,16,32]{1,4,3,2,0:T(8,128)(2,1)} %bitcast.133, f32[3,288,288]{1,2,0:T(8,128)S(1)} %broadcast_multiply_fusion.5, f32[16]{0:T(128)S(1)} %get-tuple-element.216, pred[3,288,288]{1,2,0:T(8,128)(4,1)} %or_and_fusion.2), kind=kOutput, calls=%fused_computation.22.clone.1 | convolution fusion | flops 537933568 | bytes 4838464 | tf_op jit(solution)/shard_map/while/body/eval_jaxpr/whqk,wkhe->wqhe/dot_general | solution.py:52
  179.6 4.9 %convolution_convert_fusion.3 = bf16[3,288,1536]{2,1,0:T(8,128)(2,1)} fusion(bf16[512,1536]{1,0:T(8,128)(2,1)} %get-tuple-element.213, f32[512]{0:T(512)S(1)} %get-tuple-element.212, f32[3,288]{1,0:T(4,128)S(1)} %add_rsqrt_fusion.3, f32[3,288]{1,0:T(4,128)S(1)} %broadcast_multiply_fusion.6, bf16[4,3,288,512]{3,2,1,0:T(8,128)(2,1)} %get-tuple-element.211, ...), kind=kOutput, calls=%fused_computation.11.clone.1 | convolution fusion | flops 1362493440 | bytes 5120772 | tf_op jit(solution)/shard_map/while/body/eval_jaxpr/wnd,de->wne/dot_general | solution.py:31
  184.5 4.7 %copy.126 = bf16[3,288,1536]{1,2,0:T(8,128)(2,1)} copy(bf16[3,288,1536]{2,1,0:T(8,128)(2,1)} %convolution_convert_fusion.3) | data formatting | bytes 5308416 | tf_op jit(solution)/shard_map/while/body/eval_jaxpr/convert_element_type | solution.py:33
  189.1 11.7 %fusion.125 = f32[3,16,288]{2,1,0:T(8,128)} fusion(f32[3,288,288]{1,2,0:T(8,128)S(1)} %broadcast_multiply_fusion.5, f32[16]{0:T(128)S(1)} %get-tuple-element.216, pred[3,288,288]{1,2,0:T(8,128)(4,1)} %or_and_fusion.2, bf16[3,288,3,16,32]{1,4,3,2,0:T(8,128)(2,1)} %bitcast.132), kind=kOutput, calls=%fused_computation.137.clone.1 | convolution fusion | flops 278692128 | bytes 3741760 | tf_op jit(solution)/shard_map/while/body/eval_jaxpr/sub | solution.py:50
  200.8 13.3 %fusion.126 = bf16[3,16,32,288]{3,2,1,0:T(8,128)(2,1)} fusion(f32[3,16,288]{2,1,0:T(8,128)} %fusion.125, bf16[3,288,3,16,32]{1,4,3,2,0:T(8,128)(2,1)} %bitcast.133, f32[3,288,288]{1,2,0:T(8,128)S(1)} %broadcast_multiply_fusion.5, f32[16]{0:T(128)S(1)} %get-tuple-element.216, pred[3,288,288]{1,2,0:T(8,128)(4,1)} %or_and_fusion.2), kind=kOutput, calls=%fused_computation.22.clone.1 | convolution fusion | flops 537933568 | bytes 4838464 | tf_op jit(solution)/shard_map/while/body/eval_jaxpr/whqk,wkhe->wqhe/dot_general | solution.py:52
  217.3 4.7 %copy.97 = bf16[4,3,288,512]{3,0,2,1:T(4,128)(2,1)S(1)} copy(bf16[4,3,288,512]{3,2,1,0:T(8,128)(2,1)} %get-tuple-element.57) | data formatting | bytes 7077888 | tf_op jit(solution)/shard_map/while | solution.py:87
  222.0 3.6 copy.98
  226.0 4.1 %collective-permute-start.4 = (bf16[2,6,36,512]{3,0,2,1:T(2,128)(2,1)S(1)}, bf16[2,6,36,512]{3,0,2,1:T(2,128)(2,1)S(1)}, u32[]{:S(2)}, u32[]{:S(2)}) collective-permute-start(bf16[2,6,36,512]{3,0,2,1:T(2,128)(2,1)S(1)} %slice.76), channel_id=1, source_target_pairs={{0,32},{32,64},{64,96},{96,0},{1,33},{33,65},{65,97},{97,1},{2,34}... | collective-permute-start | bytes 1327112 | tf_op jit(solution)/shard_map/ppermute | solution.py:14
  235.8 17.4 %collective-permute-done.5 = bf16[2,48,6,512]{3,1,2,0:T(8,128)(2,1)S(1)} collective-permute-done((bf16[2,48,6,512]{3,1,2,0:T(8,128)(2,1)S(1)}, bf16[2,48,6,512]{3,1,2,0:T(8,128)(2,1)S(1)}, u32[]{:S(2)}, u32[]{:S(2)}) %collective-permute-start.5) | collective-permute-done | bytes 589856 | tf_op jit(solution)/shard_map/ppermute | solution.py:14
  258.2 3.7 %multiply_convert_fusion = bf16[2,48,36,512]{3,1,2,0:T(8,128)(2,1)S(1)} fusion(bf16[2,48,36,512]{3,1,2,0:T(8,128)(2,1)S(1)} %copy-done.3, f32[512]{0:T(512)S(1)} %copy-done.11, f32[2,48,36]{1,2,0:T(8,128)S(1)} %add_rsqrt_fusion.1, f32[2,48,36]{1,2,0:T(8,128)S(1)} %broadcast_multiply_fusion.2, bf16[2,42,36,512]{3,1,2,0:T(8,128)(2,1)S(1)} %copy.111, ...), kind=kLoop, calls=%fused_computation.76 | loop fusion | flops 21233664 | bytes 11236352 | tf_op jit(solution)/shard_map/convert_element_type | solution.py:21
  261.9 3.9 %copy.101 = bf16[2,48,36,512]{3,2,1,0:T(8,128)(2,1)} copy(bf16[2,48,36,512]{3,1,2,0:T(8,128)(2,1)S(1)} %multiply_convert_fusion) | data formatting | bytes 7077888 | tf_op jit(solution)/shard_map/convert_element_type | solution.py:21
  265.8 6.2 %reshape.124 = bf16[3456,512]{1,0:T(8,128)(2,1)} reshape(bf16[2,48,36,512]{3,2,1,0:T(8,128)(2,1)} %copy.101) | data formatting | bytes 7077888 | tf_op jit(solution)/shard_map/reshape | solution.py:97
  272.1 66.7 %fusion.106 = bf16[3456,2048]{1,0:T(8,128)(2,1)S(1)} fusion(bf16[3456,512]{1,0:T(8,128)(2,1)} %reshape.124, bf16[512,2048]{1,0:T(8,128)(2,1)S(1)} %copy-done), kind=kOutput, calls=%fused_computation.56.clone.clone.1 | convolution fusion | flops 7707820032 | bytes 19791872 | tf_op jit(solution)/shard_map/dot_general | solution.py:99
  338.8 10.0 %fusion.47 = f32[3456,512]{1,0:T(8,128)} fusion(bf16[2048,512]{1,0:T(8,128)(2,1)S(1)} %copy-done.12, bf16[3456,2048]{1,0:T(8,128)(2,1)S(1)} %fusion.106), kind=kOutput, calls=%fused_computation.72 | convolution fusion | flops 7247757312 | bytes 23330816 | tf_op jit(solution)/shard_map/dot_general | solution.py:101
  348.8 8.9 %reshape.125 = f32[2,48,36,512]{3,2,1,0:T(8,128)} reshape(f32[3456,512]{1,0:T(8,128)} %fusion.47) | data formatting | bytes 14155776 | tf_op jit(solution)/shard_map/reshape | solution.py:101
  357.7 10.3 %fusion.51 = bf16[2,48,36,512]{3,1,2,0:T(8,128)(2,1)} fusion(f32[2,48,36,512]{3,2,1,0:T(8,128)} %reshape.125, bf16[2,48,36,512]{3,1,2,0:T(8,128)(2,1)} %param.12, bf16[2,42,36,512]{3,1,2,0:T(8,128)(2,1)} %copy-done.2, bf16[2,6,36,512]{3,1,2,0:T(8,128)(2,1)S(1)} %copy-done.5, bf16[2,48,6,512]{3,1,2,0:T(8,128)(2,1)S(1)} %copy-done.7), kind=kLoop, calls=%fused_computation.75 | loop fusion | flops 17694720 | bytes 18284544 | tf_op jit(solution)/shard_map/convert_element_type | solution.py:104
  (121 shorter events, 62.4 us)
Async XLA Ops:
  0.0 272.1 %copy-start = (bf16[512,2048]{1,0:T(8,128)(2,1)S(1)}, bf16[512,2048]{1,0:T(8,128)(2,1)}, u32[]{:S(2)}) copy-start(bf16[512,2048]{1,0:T(8,128)(2,1)} %param.20) | copy-start | bytes 6291460
  0.0 12.9 %copy-start.8 = (s32[48,36]{0,1:T(8,128)S(1)}, s32[48,36]{0,1:T(8,128)}, u32[]{:S(2)}) copy-start(s32[48,36]{0,1:T(8,128)} %param.14) | copy-start | bytes 20740
  0.0 12.9 %copy-start.9 = (s32[48,36]{0,1:T(8,128)S(1)}, s32[48,36]{0,1:T(8,128)}, u32[]{:S(2)}) copy-start(s32[48,36]{0,1:T(8,128)} %param.13) | copy-start | bytes 20740
  1.4 11.5 %collective-permute-start = (bf16[2,6,36,512]{3,2,1,0:T(8,128)(2,1)S(1)}, bf16[2,6,36,512]{3,2,1,0:T(8,128)(2,1)S(1)}, u32[]{:S(2)}, u32[]{:S(2)}) collective-permute-start(bf16[2,6,36,512]{3,2,1,0:T(8,128)(2,1)S(1)} %copy.110), channel_id=1, source_target_pairs={{0,96},{32,0},{64,32},{96,64},{1,97},{33,1},{65,33},{97,65},{2,98}... | collective-permute-start | bytes 1327112 | tf_op jit(solution)/shard_map/ppermute | solution.py:14
  4.3 17.7 %collective-permute-start.2 = (s32[2,6,36]{1,2,0:T(8,128)}, s32[2,6,36]{1,2,0:T(8,128)S(1)}, u32[]{:S(2)}, u32[]{:S(2)}) collective-permute-start(s32[2,6,36]{1,2,0:T(8,128)} %pad_add_fusion), channel_id=1, source_target_pairs={{0,96},{32,0},{64,32},{96,64},{1,97},{33,1},{65,33},{97,65},{2,98}... | collective-permute-start | bytes 5192 | tf_op jit(solution)/shard_map/ppermute | solution.py:14
  15.1 24.6 %collective-permute-start.1 = (bf16[2,48,6,512]{3,1,2,0:T(8,128)(2,1)}, bf16[2,48,6,512]{3,1,2,0:T(8,128)(2,1)S(1)}, u32[]{:S(2)}, u32[]{:S(2)}) collective-permute-start(bf16[2,48,6,512]{3,1,2,0:T(8,128)(2,1)} %pad_maximum_fusion.3), channel_id=1, source_target_pairs={{0,31},{1,0},{2,1},{3,2},{4,3},{5,4},{6,5},{7,6},{8,7},{9,8},{10,9... | collective-permute-start | bytes 1769480 | tf_op jit(solution)/shard_map/ppermute | solution.py:14
  22.0 11.5 %collective-permute-start.3 = (s32[2,48,6]{1,2,0:T(8,128)S(1)}, s32[2,48,6]{1,2,0:T(8,128)S(1)}, u32[]{:S(2)}, u32[]{:S(2)}) collective-permute-start(s32[2,48,6]{1,2,0:T(8,128)S(1)} %pad_add_fusion.2), channel_id=1, source_target_pairs={{0,31},{1,0},{2,1},{3,2},{4,3},{5,4},{6,5},{7,6},{8,7},{9,8},{10,9... | collective-permute-start | bytes 6920 | tf_op jit(solution)/shard_map/ppermute | solution.py:14
  43.7 5.3 %copy-start.10 = (s32[4,288]{1,0:T(4,128)S(1)}, s32[4,288]{1,0:T(4,128)}, u32[]{:S(2)}) copy-start(s32[4,288]{1,0:T(4,128)} %broadcast_in_dim.25) | copy-start | bytes 13828
  43.7 5.3 %copy-start.13 = (f32[512]{0:T(512)S(1)}, f32[512]{0:T(512)}, u32[]{:S(2)}) copy-start(f32[512]{0:T(512)} %param.15) | copy-start | bytes 6148
  43.7 5.3 %copy-start.14 = (f32[16]{0:T(128)S(1)}, f32[16]{0:T(128)}, u32[]{:S(2)}) copy-start(f32[16]{0:T(128)} %param.17) | copy-start | bytes 196
  226.0 9.4 %collective-permute-start.4 = (bf16[2,6,36,512]{3,0,2,1:T(2,128)(2,1)S(1)}, bf16[2,6,36,512]{3,0,2,1:T(2,128)(2,1)S(1)}, u32[]{:S(2)}, u32[]{:S(2)}) collective-permute-start(bf16[2,6,36,512]{3,0,2,1:T(2,128)(2,1)S(1)} %slice.76), channel_id=1, source_target_pairs={{0,32},{32,64},{64,96},{96,0},{1,33},{33,65},{65,97},{97,1},{2,34}... | collective-permute-start | bytes 1327112 | tf_op jit(solution)/shard_map/ppermute | solution.py:14
  232.2 20.9 %copy-start.3 = (bf16[2,48,36,512]{3,1,2,0:T(8,128)(2,1)S(1)}, bf16[2,48,36,512]{3,1,2,0:T(8,128)(2,1)}, u32[]{:S(2)}) copy-start(bf16[2,48,36,512]{3,1,2,0:T(8,128)(2,1)} %param.12) | copy-start | bytes 10616836
  233.4 24.8 %copy-start.2 = (bf16[2,42,36,512]{3,1,2,0:T(8,128)(2,1)}, bf16[2,42,36,512]{3,1,2,0:T(8,128)(2,1)S(1)}, u32[]{:S(2)}) copy-start(bf16[2,42,36,512]{3,1,2,0:T(8,128)(2,1)S(1)} %copy.111) | copy-start | bytes 9289732
  235.5 22.7 %copy-start.4 = (bf16[2,6,36,512]{3,1,2,0:T(8,128)(2,1)}, bf16[2,6,36,512]{3,1,2,0:T(8,128)(2,1)S(1)}, u32[]{:S(2)}) copy-start(bf16[2,6,36,512]{3,1,2,0:T(8,128)(2,1)S(1)} %copy.100) | copy-start | bytes 1327108
  235.7 22.6 %copy-start.11 = (f32[512]{0:T(512)S(1)}, f32[512]{0:T(512)}, u32[]{:S(2)}) copy-start(f32[512]{0:T(512)} %param.19) | copy-start | bytes 6148
  235.7 17.4 %collective-permute-start.5 = (bf16[2,48,6,512]{3,1,2,0:T(8,128)(2,1)S(1)}, bf16[2,48,6,512]{3,1,2,0:T(8,128)(2,1)S(1)}, u32[]{:S(2)}, u32[]{:S(2)}) collective-permute-start(bf16[2,48,6,512]{3,1,2,0:T(8,128)(2,1)S(1)} %pad_maximum_fusion.2), channel_id=1, source_target_pairs={{0,1},{1,2},{2,3},{3,4},{4,5},{5,6},{6,7},{7,8},{8,9},{9,10},{10,1... | collective-permute-start | bytes 1769480 | tf_op jit(solution)/shard_map/ppermute | solution.py:14
  253.1 5.1 %copy-start.6 = (bf16[2,48,6,512]{3,1,2,0:T(8,128)(2,1)}, bf16[2,48,6,512]{3,1,2,0:T(8,128)(2,1)S(1)}, u32[]{:S(2)}) copy-start(bf16[2,48,6,512]{3,1,2,0:T(8,128)(2,1)S(1)} %collective-permute-done.5) | copy-start | bytes 1769476
  272.1 66.7 %copy-start.12 = (bf16[2048,512]{1,0:T(8,128)(2,1)S(1)}, bf16[2048,512]{1,0:T(8,128)(2,1)}, u32[]{:S(2)}) copy-start(bf16[2048,512]{1,0:T(8,128)(2,1)} %param.21) | copy-start | bytes 6291460
  348.8 8.9 %copy-start.5 = (bf16[2,6,36,512]{3,1,2,0:T(8,128)(2,1)S(1)}, bf16[2,6,36,512]{3,1,2,0:T(8,128)(2,1)}, u32[]{:S(2)}) copy-start(bf16[2,6,36,512]{3,1,2,0:T(8,128)(2,1)} %copy-done.4) | copy-start | bytes 1327108
  348.8 8.9 %copy-start.7 = (bf16[2,48,6,512]{3,1,2,0:T(8,128)(2,1)S(1)}, bf16[2,48,6,512]{3,1,2,0:T(8,128)(2,1)}, u32[]{:S(2)}) copy-start(bf16[2,48,6,512]{3,1,2,0:T(8,128)(2,1)} %copy-done.6) | copy-start | bytes 1769476
  348.8 19.2 %copy-start.1 = (bf16[512,2048]{1,0:T(8,128)(2,1)S(1)}, bf16[512,2048]{1,0:T(8,128)(2,1)}, u32[]{:S(2)}) copy-start(bf16[512,2048]{1,0:T(8,128)(2,1)} %param.20) | copy-start | bytes 6291460
where the time goes:
time: 375 us; the launch traced here: 368 us
  matrix products  208 us (55%)
  local copies, waits for them, and re-layouts  70.9 us (19%)
  other arithmetic  42.8 us (11%)
  waiting for transfers between devices  30.4 us (8%)
  starting transfers between devices  14.8 us (4%)
    dot_general x1, matrix products, feed_forward(): jnp.dot(normed, up_weight, preferred_element_type=jnp.float32)  66.7 us
    dot_general x4, matrix products, attend_windows(): jnp.einsum('whqk,wkhe->wqhe', attn_weights, val_rows, preferred_element_t...  53.2 us
    sub x4, matrix products, attend_windows(): raised = jnp.exp(scores - row_max)  46.8 us
    ppermute x6, waiting for transfers between devices, from_behind(): lax.ppermute(value, axis, [(i, (i + by) % devices) for i in range(devices)])  30.4 us
    dot_general x4, matrix products, attend_windows(): jnp.einsum('wnd,de->wne', normed, qkv_weight, preferred_element_type=jnp....  19.5 us
    convert_element_type x4, local copies, waits for them, and re-layouts, attend_windows(): packed = jnp.einsum('wnd,de->wne', normed, qkv_weight, preferred_element_...  18.7 us
    ppermute x6, starting transfers between devices, from_behind(): lax.ppermute(value, axis, [(i, (i + by) % devices) for i in range(devices)])  14.8 us
    dot_general x4, matrix products, attend_windows(): jnp.einsum('wnd,de->wne', heads_out, out_weight, preferred_element_type=j...  11.8 us
  transfers between devices with their start and end apart: 6, of which 3 were waited for; matrix products, arithmetic and copies ran while one was open for 5% of the time, Pallas kernels for 0%

commit v1 on v0

v1 whole, which is shorter than its diff:
```python
import math, functools
import jax, jax.numpy as jnp
from jax import lax
from jax.experimental import pallas as pl
from jax.experimental.pallas import tpu as pltpu

F32, BF16 = jnp.float32, jnp.bfloat16
LOG2E = math.log2(math.e)
D, HEADS, FF = 512, 16, 2048
SCALE = LOG2E / math.sqrt(32.0)
W = 288
NEG = -1e30

def dot(a, b):
    return lax.dot_general(a, b, (((1,), (0,)), ((), ())), preferred_element_type=F32)

def dot_t(a, b):
    return lax.dot_general(a, b, (((1,), (1,)), ((), ())), preferred_element_type=F32)

def norm(x, g):
    c = x - jnp.mean(x, axis=-1, keepdims=True)
    s = jnp.mean(c * c, axis=-1, keepdims=True)
    return c * lax.rsqrt(s + 1e-5) * g

def lanes(shape):
    return lax.broadcasted_iota(jnp.int32, shape, len(shape) - 1)

def rows(shape):
    return lax.broadcasted_iota(jnp.int32, shape, len(shape) - 2)

def gelu(x):
    return 0.5 * x * (1.0 + lax.erf(x * (1 / math.sqrt(2.0))))

def split3(v):
    hi = v.astype(BF16).astype(F32)
    mid = (v - hi).astype(BF16).astype(F32)
    return hi, mid, v - hi - mid

def bias_lanes(b, n):
    hi, mid, lo = split3(jnp.full((1, 128), b * LOG2E, F32))
    at = lanes((1, 128))
    return jnp.where(at == 0, hi, jnp.where(at == 1, mid, jnp.where(at == 2, lo, 0.0)))

def attend(nq, q_of, k_of, v_of, land_q, land_k, mask, mask_tail, bias_ref, qs, ke, kt, s_ref, t_ref, p_ref, ve, heads_out, ho_row):
    seg = lanes((1, 128)) // 32
    three = (lanes((1, 128)) < 3).astype(F32)
    for g in range(4):
        b = g % 2
        q = q_of(g)
        k = k_of(g)
        v = v_of(g)
        kland = (land_k * three).astype(BF16)
        ke[b, :, 0:128] = k
        ke[b, :, 128:256] = kland
        qland = land_q
        for h in range(4):
            hm = (seg == h)
            qs[b, h * nq:(h + 1) * nq, 0:128] = jnp.where(hm, q, 0.0).astype(BF16)
            qs[b, h * nq:(h + 1) * nq, 128:256] = (qland * bias_lanes(bias_ref[4 * g + h], 128)).astype(BF16)
            hmb = hm.astype(BF16)
            ve[b, h * 256:(h + 1) * 256, 0:128] = v[0:256] * hmb
            ve[b, h * 256:(h + 1) * 256, 128:256] = jnp.broadcast_to(hmb, (256, 128))
            ve[b, 1024 + 32 * h:1056 + 32 * h, 0:128] = v[256:288] * hmb
            ve[b, 1024 + 32 * h:1056 + 32 * h, 128:256] = jnp.broadcast_to(hmb, (32, 128))
            kt[b, 32 * h:32 * h + 32, 0:128] = k[256:288] * hmb
            kt[b, 32 * h:32 * h + 32, 128:256] = (land_k[256:288] * bias_lanes(bias_ref[4 * g + h], 128)).astype(BF16)
        qs[b, 4 * nq:5 * nq, 0:128] = q.astype(BF16)
        qs[b, 4 * nq:5 * nq, 128:256] = (land_q * three).astype(BF16)
        s_ref[b, 0:4 * nq] = dot_t(qs[b, 0:4 * nq], ke[b, 0:256])
        t_ref[b, 0:nq] = dot_t(qs[b, 4 * nq:5 * nq], kt[b])
        R = 16
        for r in range(0, nq, R):
            rr = min(R, nq - r)
            t = t_ref[b, r:r + rr] + mask_tail[r:r + rr]
            mk = mask[r:r + rr]
            ms = []
            for h in range(4):
                s = s_ref[b, h * nq + r:h * nq + r + rr] + mk
                m = jnp.maximum(jnp.maximum(s[:, :128], s[:, 128:]), jnp.where(seg == h, t, -3e38))
                m = jnp.max(m, axis=-1, keepdims=True)
                p_ref[b, r:r + rr, h * 256:(h + 1) * 256] = jnp.exp2(s - m).astype(BF16)
                ms.append(m)
            mt = jnp.where(seg == 0, ms[0], jnp.where(seg == 1, ms[1], jnp.where(seg == 2, ms[2], ms[3])))
            p_ref[b, r:r + rr, 1024:1152] = jnp.exp2(t - mt).astype(BF16)
        o = dot(p_ref[b, 0:nq], ve[b])
        heads_out[pl.ds(ho_row, nq), g * 128:(g + 1) * 128] = (o[:, :128] / o[:, 128:]).astype(BF16)

def k1_body(x, land, pad, g1, wqkv, bias, wout, g2, wup, wdown, out, edge, xg, qkv, ho, qs, ke, kt, s_ref, t_ref, p_ref, ve, mk, mkt, att, nat, skip=()):
    gain1 = g1[...]
    if "ln" not in skip:
      @pl.loop(0, 24)
      def _(n):
        l, m = n // 12, n % 12
        jc, p = m // 6, m % 6
        for two in range(2):
            v = norm(x[l, 6 + jc * 12 + 2 * p + two].astype(F32), gain1)
            for i in range(3):
                w = jc * 3 + i
                row = pl.multiple_of(l * 144 + 24 * p, 8)
                xg.at[w, pl.ds(row, 24), :][12 * two:12 * two + 12, :] = v[6 + 12 * i:18 + 12 * i]
    if "qkv" not in skip:
      @pl.loop(0, 6)
      def _(w):
        xn = xg[w].astype(BF16)
        for c in range(6):
            r = dot(xn, wqkv[:, c * 256:(c + 1) * 256])
            if c < 2:
                r = r * SCALE
            qkv[w, :, c * 256:(c + 1) * 256] = r.astype(BF16)
    if "att" not in skip:
      @pl.loop(0, 6)
      def _(w):
        jc, i = w // 3, w % 3
        at_c = rows((36, W))
        lane = lanes((1, W)) % 144
        here = at_c == (6 + jc * 12 + lane // 12)
        pick = (rows((48, W)) == (6 + i * 12 + lane % 12)).astype(BF16)
        landrow = jnp.sum(jnp.where(here, dot(land[...].astype(F32).astype(BF16), pick), 0.0), axis=0, keepdims=True)
        padrow = jnp.sum(jnp.where(here, dot(pad[...].astype(F32).astype(BF16), pick), 0.0), axis=0, keepdims=True)
        eye = rows((W, W)) == lanes((W, W))
        land_k = jnp.broadcast_to(jnp.sum(jnp.where(eye, landrow, 0.0), axis=1, keepdims=True), (W, 128))
        mm = jnp.where(eye, 0.0, padrow * NEG)
        mk[...] = mm[:, 0:256]
        mkt[...] = jnp.concatenate([mm[:, 256:288]] * 4, axis=1)
        attend(W, lambda g: qkv[w, :, g * 128:(g + 1) * 128].astype(F32),
               lambda g: qkv[w, :, 512 + g * 128:512 + (g + 1) * 128],
               lambda g: qkv[w, :, 1024 + g * 128:1024 + (g + 1) * 128],
               land_k, land_k, mk, mkt, bias, qs, ke, kt, s_ref, t_ref, p_ref, ve, ho, pl.multiple_of(w * W, 32))
    if "op" not in skip:
      @pl.loop(0, 6)
      def _(w):
        h = ho[pl.ds(pl.multiple_of(w * W, 32), W), :]
        for c in range(2):
            att[w, :, c * 256:(c + 1) * 256] = dot(h, wout[:, c * 256:(c + 1) * 256])
    if "sc" not in skip:
      @pl.loop(0, 24)
      def _(n):
        l, m = n // 12, n % 12
        jc, p = m // 6, m % 6
        for two in range(2):
            c = jc * 12 + 2 * p + two
            for i in range(3):
                w = jc * 3 + i
                row = pl.multiple_of(l * 144 + 24 * p, 8)
                nat[l * 24 + c, 6 + 12 * i:18 + 12 * i, :] = att.at[w, pl.ds(row, 24), :][12 * two:12 * two + 12, :]
            nat[l * 24 + c] = nat[l * 24 + c] + x[l, 6 + c].astype(F32)
            edge[l * 24 + c, 0] = nat[l * 24 + c, 0:8]
            edge[l * 24 + c, 1] = nat[l * 24 + c, 40:48]
    gain2 = g2[...]
    if "ffn" not in skip:
      CH = 12
      @pl.loop(0, 48 // CH)
      def _(n):
        res = nat[pl.ds(n * CH, CH), 8:40, :].reshape(CH * 32, 512)
        xn = norm(res, gain2).astype(BF16)
        acc = res
        for c in range(4):
            hid = gelu(dot(xn, wup[:, c * 512:(c + 1) * 512])).astype(BF16)
            acc = acc + dot(hid, wdown[c * 512:(c + 1) * 512, :])
        out[pl.ds(n * CH, CH)] = acc.astype(BF16).reshape(CH, 32, 512)

def k1(xt, landt, padt, g1, wqkv, bias, wout, g2, wup, wdown, skip=()):
    vm = pl.BlockSpec(memory_space=pltpu.VMEM)
    sm = pl.BlockSpec(memory_space=pltpu.SMEM)
    return pl.pallas_call(
        functools.partial(k1_body, skip=skip),
        out_shape=[jax.ShapeDtypeStruct((48, 32, 512), BF16), jax.ShapeDtypeStruct((48, 2, 8, 512), F32)],
        in_specs=[vm, vm, vm, vm, vm, sm, vm, vm, vm, vm],
        out_specs=[vm, vm],
        scratch_shapes=[
            pltpu.VMEM((6, W, 512), F32),
            pltpu.VMEM((6, W, 1536), BF16),
            pltpu.VMEM((6 * W, 512), BF16),
            pltpu.VMEM((2, 5 * W, 256), BF16),
            pltpu.VMEM((2, W, 256), BF16),
            pltpu.VMEM((2, 128, 256), BF16),
            pltpu.VMEM((2, 4 * W, 256), F32),
            pltpu.VMEM((2, W, 128), F32),
            pltpu.VMEM((2, W, 1152), BF16),
            pltpu.VMEM((2, 1152, 256), BF16),
            pltpu.VMEM((W, 256), F32),
            pltpu.VMEM((W, 128), F32),
            pltpu.VMEM((6, W, 512), F32),
            pltpu.VMEM((48, 48, 512), F32),
        ],
        compiler_params=pltpu.CompilerParams(vmem_limit_bytes=60 * 1024 * 1024),
    )(xt, landt, padt, g1.reshape(1, 512), wqkv, bias, wout, g2.reshape(1, 512), wup, wdown)

import numpy as np
from jax.sharding import PartitionSpec as P


def edge_windows():
    tens = [(i, j) for i in (1, 2, 3) for j in (0, 3)] + [(i, j) for i in (0, 4) for j in (1, 2)]
    return tens + [(i, j) for i in (0, 4) for j in (0, 3)]


def pieces(i, j):
    halves = {0: ((6, 6), (0, 6)), 4: ((48, 6), (54, 6))}.get(i, ((12 * i, 12),))
    cols = {0: (range(6, 12), range(0, 6)), 3: (range(36, 42), range(42, 48))}.get(j, (range(12 * j, 12 * j + 12),))
    return [(l, e, f, n) for es in cols for f, n in halves for l in range(2) for e in es]


def cell_maps():
    e_of, f_of = [], []
    for i, j in edge_windows():
        e_of.append([e for l, e, f, n in pieces(i, j) for _ in range(n)])
        f_of.append([f + a for l, e, f, n in pieces(i, j) for a in range(n)])
    return np.array(e_of, np.int32)[:, None], np.array(f_of, np.int32)[:, None]


def k2_body(flags, e_map, f_map, land, pad, x, left, right, up, down, ul, ur, dl, dr, inner, edge,
            g1, wqkv, bias, wout, g2, wup, wdown, out,
            xg, qkv, ho, qs, ke, kt, s_ref, t_ref, p_ref, ve, mk, mkt, att, nat_s, nat_i):
    wins = edge_windows()

    def column(l, e, f):
        if f < 6:
            return (ul, l, e) if e < 6 else (up, l, e - 6) if e < 42 else (ur, l, e - 42)
        if f >= 54:
            return (dl, l, e) if e < 6 else (down, l, e - 6) if e < 42 else (dr, l, e - 42)
        return (left, l, e) if e < 6 else (x, l, e - 6) if e < 42 else (right, l, e - 42)

    for w, (i, j) in enumerate(wins):
        row = 0
        for l, e, f, n in pieces(i, j):
            ref, a, b = column(l, e, f)
            start = 0 if f < 6 or f >= 54 else f - 6
            xg[w, row:row + n, :] = ref[a, b].astype(F32)[start:start + n]
            row += n
    gain1 = g1[...]

    @pl.loop(0, 14)
    def _(w):
        xn = norm(xg[w], gain1).astype(BF16)
        for c in range(2):
            qkv[w, 0:144, c * 256:(c + 1) * 256] = (dot(xn[0:144], wqkv[:, c * 256:(c + 1) * 256]) * SCALE).astype(BF16)
        for c in range(2, 6):
            qkv[w, :, c * 256:(c + 1) * 256] = dot(xn, wqkv[:, c * 256:(c + 1) * 256]).astype(BF16)

    def window(w, nq):
        here = rows((48, W)) == e_map[w]
        pick = (rows((64, W)) == f_map[w]).astype(BF16)
        landrow = jnp.sum(jnp.where(here, dot(land[...].astype(F32).astype(BF16), pick), 0.0), axis=0, keepdims=True)
        padrow = jnp.sum(jnp.where(here, dot(pad[...].astype(F32).astype(BF16), pick), 0.0), axis=0, keepdims=True)
        f_row = f_map[w]
        over = ((f_row < 6) & (flags[0] > 0)) | ((f_row >= 54) & (flags[1] > 0))
        blocked = jnp.where(over | (padrow > 0.5), NEG, 0.0)
        eye = rows((W, W)) == lanes((W, W))
        land_k = jnp.broadcast_to(jnp.sum(jnp.where(eye, landrow, 0.0), axis=1, keepdims=True), (W, 128))
        mm = jnp.where(rows((nq, W)) == lanes((nq, W)), 0.0, blocked)
        mk[0:nq] = mm[:, 0:256]
        mkt[0:nq] = jnp.concatenate([mm[:, 256:288]] * 4, axis=1)
        attend(nq, lambda g: qkv[w, 0:nq, g * 128:(g + 1) * 128].astype(F32),
               lambda g: qkv[w, :, 512 + g * 128:512 + (g + 1) * 128],
               lambda g: qkv[w, :, 1024 + g * 128:1024 + (g + 1) * 128],
               land_k[0:nq], land_k, mk, mkt, bias, qs, ke, kt, s_ref, t_ref, p_ref, ve, ho, pl.multiple_of(w * 144, 16))

    @pl.loop(0, 10)
    def _(w):
        window(w, 144)

    @pl.loop(10, 14)
    def _(w):
        window(w, 72)

    @pl.loop(0, 7)
    def _(n):
        h = ho[pl.ds(pl.multiple_of(n * 288, 32), 288), :]
        for c in range(2):
            a = dot(h, wout[:, c * 256:(c + 1) * 256])
            att[2 * n, :, c * 256:(c + 1) * 256] = a[0:144]
            att[2 * n + 1, :, c * 256:(c + 1) * 256] = a[144:288]

    side = {c: s for s, c in enumerate(list(range(6)) + list(range(30, 36)))}
    for w, (i, j) in enumerate(wins):
        row = 0
        for l, e, f, n in pieces(i, j):
            if row == (144 if w < 10 else 72):
                break
            c, r = e - 6, f - 6
            seg = att[w, row:row + n, :]
            if c in side:
                nat_s[l * 12 + side[c], r:r + n, :] = seg
            elif r == 0:
                nat_i[l * 24 + c - 6, 0, 0:6, :] = seg
            else:
                nat_i[l * 24 + c - 6, 1, 2:8, :] = seg
            row += n
    gain2 = g2[...]

    def ffn(res):
        xn = norm(res, gain2).astype(BF16)
        acc = res
        for c in range(4):
            hid = gelu(dot(xn, wup[:, c * 512:(c + 1) * 512])).astype(BF16)
            acc = acc + dot(hid, wdown[c * 512:(c + 1) * 512, :])
        return acc.astype(BF16)

    @pl.loop(0, 4)
    def _(n):
        l = n // 2
        c0 = 30 * (n % 2)
        res = nat_s[pl.ds(6 * n, 6)] + x[l, pl.ds(c0, 6)].astype(F32)
        out[l, pl.ds(c0, 6)] = ffn(res.reshape(288, 512)).reshape(6, 48, 512)

    @pl.loop(0, 4)
    def _(n):
        l = n // 2
        c0 = 12 * (n % 2)
        xs = x[l, pl.ds(6 + c0, 12)].astype(F32)
        at = nat_i[pl.ds(12 * n, 12)]
        ed = edge[pl.ds(12 * n, 12)]
        low = jnp.where(rows((1, 8, 512)) < 6, at[:, 0] + xs[:, 0:8], ed[:, 0])
        high = jnp.where(rows((1, 8, 512)) >= 2, at[:, 1] + xs[:, 40:48], ed[:, 1])
        res = jnp.concatenate([low.reshape(96, 512), high.reshape(96, 512)], axis=0)
        y = ffn(res).astype(F32)
        full = jnp.concatenate([y[0:96].reshape(12, 8, 512), inner[pl.ds(12 * n, 12)].astype(F32), y[96:192].reshape(12, 8, 512)], axis=1)
        out[l, pl.ds(6 + c0, 12)] = full.astype(BF16)


def k2(flags, land, pad, xt, halos, inner, edge, g1, wqkv, bias, wout, g2, wup, wdown):
    vm = pl.BlockSpec(memory_space=pltpu.VMEM)
    sm = pl.BlockSpec(memory_space=pltpu.SMEM)
    e_map, f_map = cell_maps()
    return pl.pallas_call(
        k2_body,
        out_shape=jax.ShapeDtypeStruct((2, 36, 48, 512), BF16),
        in_specs=[sm] + [vm] * 17 + [sm] + [vm] * 4,
        out_specs=vm,
        scratch_shapes=[
            pltpu.VMEM((14, W, 512), F32),
            pltpu.VMEM((14, W, 1536), BF16),
            pltpu.VMEM((14 * 144, 512), BF16),
            pltpu.VMEM((2, 5 * 144, 256), BF16),
            pltpu.VMEM((2, W, 256), BF16),
            pltpu.VMEM((2, 128, 256), BF16),
            pltpu.VMEM((2, 4 * 144, 256), F32),
            pltpu.VMEM((2, 144, 128), F32),
            pltpu.VMEM((2, 144, 1152), BF16),
            pltpu.VMEM((2, 1152, 256), BF16),
            pltpu.VMEM((144, 256), F32),
            pltpu.VMEM((144, 128), F32),
            pltpu.VMEM((14, 144, 512), F32),
            pltpu.VMEM((24, 48, 512), F32),
            pltpu.VMEM((48, 2, 8, 512), F32),
        ],
        compiler_params=pltpu.CompilerParams(vmem_limit_bytes=62 * 1024 * 1024),
    )(flags, jnp.asarray(e_map), jnp.asarray(f_map), land, pad, xt, *halos, inner, edge,
      g1.reshape(1, 512), wqkv, bias, wout, g2.reshape(1, 512), wup, wdown)


def from_behind(value, axis, by):
    devices = lax.axis_size(axis)
    return lax.ppermute(value, axis, [(i, (i + by) % devices) for i in range(devices)])


def from_corner(value, by_lat, by_lon):
    n, m = lax.axis_size("lat"), lax.axis_size("lon")
    pairs = [(a * m + b, (a + by_lat) % n * m + (b + by_lon) % m) for a in range(n) for b in range(m)]
    return lax.ppermute(value, ("lat", "lon"), pairs)


def on_device(latent_field, land_mask, padded, norm1_gain, qkv_weight, land_bias, out_weight, norm2_gain, up_weight, down_weight):
    xt = latent_field.transpose(0, 2, 1, 3)
    masks = jnp.stack([land_mask.T, padded.T])
    left = from_behind(xt[:, 30:36], "lon", 1)
    right = from_behind(xt[:, 0:6], "lon", -1)
    up = from_behind(xt[:, :, 42:48], "lat", 1)
    down = from_behind(xt[:, :, 0:6], "lat", -1)
    ul = from_corner(xt[:, 30:36, 42:48], 1, 1)
    ur = from_corner(xt[:, 0:6, 42:48], 1, -1)
    dl = from_corner(xt[:, 30:36, 0:6], -1, 1)
    dr = from_corner(xt[:, 0:6, 0:6], -1, -1)
    tall = jnp.concatenate([from_behind(masks[:, :, 42:48], "lat", 1), masks, from_behind(masks[:, :, 0:6], "lat", -1)], 2)
    wide = jnp.concatenate([from_behind(tall[:, 30:36], "lon", 1), tall, from_behind(tall[:, 0:6], "lon", -1)], 1)
    wide = jnp.pad(wide, ((0, 0), (0, 0), (0, 4)))
    lat = lax.axis_index("lat")
    flags = jnp.stack([(lat == 0).astype(jnp.int32), (lat == lax.axis_size("lat") - 1).astype(jnp.int32)])
    inner, edge = k1(xt, masks[0], masks[1], norm1_gain, qkv_weight, land_bias, out_weight, norm2_gain, up_weight, down_weight)
    y = k2(flags, wide[0], wide[1], xt, (left, right, up, down, ul, ur, dl, dr), inner, edge,
           norm1_gain, qkv_weight, land_bias, out_weight, norm2_gain, up_weight, down_weight)
    return y.transpose(0, 2, 1, 3)


def solution(mesh):
    spec = P(None, "lat", "lon", None)
    placed = (spec, P("lat", "lon"), P("lat", "lon")) + (P(),) * 7
    return jax.shard_map(on_device, mesh=mesh, in_specs=placed, out_specs=spec, check_vma=False)
```

time: 375 us -> 183 us (0.49); the launches traced: 368 us -> 183 us
  matrix products: 208 us -> 0 us
  Pallas kernels: 0 us -> 121 us
  local copies, waits for them, and re-layouts: 70.9 us -> 11.4 us
  other arithmetic: 42.8 us -> 1.69 us
  starting transfers between devices: 14.8 us -> 22.7 us
  waiting for transfers between devices: 30.4 us -> 26.4 us
    dot_general x14 -> x0, matrix products: 161 us -> none  [the longest x1 66.7 us: feed_forward(): jnp.dot(normed, up_weight, preferred_element_type=jnp.float32)]
    pallas_call x0 -> x2, Pallas kernels: none -> 121 us  [the longest x1 70.3 us: k2(): pl.pallas_call(k2_body, out_shape=jax.ShapeDtypeStruct((2, 36, 48, 512),...]
    sub x4 -> x0, matrix products: 46.8 us -> none  [attend_windows(): raised = jnp.exp(scores - row_max)]
    convert_element_type x5 -> x0, local copies, waits for them, and re-layouts: 22.6 us -> none  [the longest x4 18.7 us: attend_windows(): packed = jnp.einsum('wnd,de->wne', normed, qkv_weight, preferred_element_...]
    reduce_sum x10 -> x0, other arithmetic: 17.2 us -> none  [the longest x5 9.44 us: layer_norm(): spread = jnp.mean(center * center, axis=-1, keepdims=True)]
    reshape x4 -> x0, local copies, waits for them, and re-layouts: 15.4 us -> none  [the longest x1 8.9 us: feed_forward(): jnp.dot(hidden, down_weight, preferred_element_type=jnp.float32)]
    ppermute x6 -> x8, waiting for transfers between devices: 30.4 us -> 15.7 us  [from_behind(): lax.ppermute(value, axis, [(i, (i + by) % devices) for i in range(devices)])]
    convert_element_type x7 -> x0, other arithmetic: 14 us -> none  [the longest x1 10.3 us: feed_forward(): return output.astype(jnp.bfloat16)]
  transfers between devices with their start and end apart: 6 -> 12, of which waited for: 3 -> 3; matrix products, arithmetic and copies ran while one was open for 5% -> 6% of each run, Pallas kernels for 0% -> 28%
where the time goes in v1:
time: 183 us
  Pallas kernels  121 us (66%)
  waiting for transfers between devices  26.4 us (14%)
  starting transfers between devices  22.7 us (12%)
  local copies, waits for them, and re-layouts  11.4 us (6%)
    pallas_call x1, Pallas kernels, k2(): pl.pallas_call(k2_body, out_shape=jax.ShapeDtypeStruct((2, 36, 48, 512),...  70.3 us
    pallas_call x1, Pallas kernels, k1(): pl.pallas_call(functools.partial(k1_body, skip=skip), out_shape=[jax.Shap...  50.3 us
    ppermute x8, waiting for transfers between devices, from_behind(): lax.ppermute(value, axis, [(i, (i + by) % devices) for i in range(devices)])  15.7 us
    ppermute x8, starting transfers between devices, from_behind(): lax.ppermute(value, axis, [(i, (i + by) % devices) for i in range(devices)])  13.7 us
    ppermute x4, waiting for transfers between devices, from_corner(): return lax.ppermute(value, ('lat', 'lon'), pairs)  10.8 us
    ppermute x4, starting transfers between devices, from_corner(): return lax.ppermute(value, ('lat', 'lon'), pairs)  8.94 us
  transfers between devices with their start and end apart: 12, of which 3 were waited for; matrix products, arithmetic and copies ran while one was open for 6% of the time, Pallas kernels for 28%

profile of v1, /device:TPU:1, one launch (start us, length us, event | category | flops | bytes accessed | tf_op | source)
XLA Modules:
  0.0 182.9 jit_solution(1937069893557669953)
XLA Ops:
  0.0 0.9 slice_add_fusion
  0.9 4.3 %collective-permute-start = (s32[2,36,6]{2,1,0:T(8,128)S(1)}, s32[2,36,6]{2,1,0:T(8,128)S(1)}, u32[]{:S(2)}, u32[]{:S(2)}) collective-permute-start(s32[2,36,6]{2,1,0:T(8,128)S(1)} %get-tuple-element.21), channel_id=1, source_target_pairs={{0,32},{32,64},{64,96},{96,0},{1,33},{33,65},{65,97},{97,1},{2,34}... | collective-permute-start | bytes 5192 | tf_op jit(solution)/shard_map/ppermute | solution.py:355
  5.2 0.0 collective-permute-start.1
  5.3 1.4 fusion.3
  6.7 1.2 copy.13
  7.9 3.2 %collective-permute-start.6 = (bf16[2,36,6,512]{3,0,2,1:T(2,128)(2,1)}, bf16[2,36,6,512]{3,0,2,1:T(2,128)(2,1)S(1)}, u32[]{:S(2)}, u32[]{:S(2)}) collective-permute-start(bf16[2,36,6,512]{3,0,2,1:T(2,128)(2,1)} %copy.13), channel_id=1, source_target_pairs={{0,32},{32,64},{64,96},{96,0},{1,33},{33,65},{65,97},{97,1},{2,34}... | collective-permute-start | bytes 1327112 | tf_op jit(solution)/shard_map/ppermute | solution.py:355
  11.1 1.2 copy.14
  12.3 0.0 collective-permute-start.7
  12.3 1.3 fusion.4
  13.7 6.1 %collective-permute-start.5 = (bf16[2,6,48,512]{3,2,1,0:T(8,128)(2,1)S(1)}, bf16[2,6,48,512]{3,2,1,0:T(8,128)(2,1)S(1)}, u32[]{:S(2)}, u32[]{:S(2)}) collective-permute-start(bf16[2,6,48,512]{3,2,1,0:T(8,128)(2,1)S(1)} %get-tuple-element.15), channel_id=1, source_target_pairs={{0,31},{1,0},{2,1},{3,2},{4,3},{5,4},{6,5},{7,6},{8,7},{9,8},{10,9... | collective-permute-start | bytes 1769480 | tf_op jit(solution)/shard_map/ppermute | solution.py:355
  19.8 0.1 pad_add_fusion.5
  19.9 0.0 collective-permute-start.2
  19.9 1.8 fusion.2
  21.7 15.7 %collective-permute-done.2 = s32[2,6,60]{2,1,0:T(8,128)S(1)} collective-permute-done((s32[2,6,60]{2,1,0:T(8,128)S(1)}, s32[2,6,60]{2,1,0:T(8,128)S(1)}, u32[]{:S(2)}, u32[]{:S(2)}) %collective-permute-start.2) | collective-permute-done | bytes 2912 | tf_op jit(solution)/shard_map/ppermute | solution.py:355
  37.4 0.6 add_convert_fusion.flags
  38.0 50.3 %shard_map.118 = (bf16[48,32,512]{2,1,0:T(8,128)(2,1)}, f32[48,2,8,512]{3,2,1,0:T(8,128)}) custom-call(bf16[2,36,48,512]{3,2,1,0:T(8,128)(2,1)} %bitcast.19, s32[36,48]{1,0:T(8,128)} %bitcast.26, s32[36,48]{1,0:T(8,128)} %bitcast.22, f32[1,512]{1,0:T(1,128)} %bitcast.29, bf16[512,1536]{1,0:T(8,128)(2,1)} %wqkv.3, f32[16]{0:T(128)} %bias.3, ...), custom_call_target="tpu_custom_call" | custom-call | tf_op jit(solution)/shard_map/pallas_call | solution.py:165
  88.3 0.0 collective-permute-done.3
  88.3 1.8 collective-permute-start.11
  90.1 0.1 pad_add_fusion
  90.2 6.0 %collective-permute-done.11.dr = bf16[2,6,6,512]{3,2,1,0:T(8,128)(2,1)S(1)} collective-permute-done((bf16[2,6,6,512]{3,2,1,0:T(8,128)(2,1)S(1)}, bf16[2,6,6,512]{3,2,1,0:T(8,128)(2,1)S(1)}, u32[]{:S(2)}, u32[]{:S(2)}) %collective-permute-start.11) | collective-permute-done | bytes 73760 | tf_op jit(solution)/shard_map/ppermute | solution.py:361
  96.2 1.5 collective-permute-start.10
  97.7 0.0 collective-permute-done.6
  97.7 5.7 %collective-permute-start.9 = (bf16[2,6,6,512]{3,2,1,0:T(8,128)(2,1)}, bf16[2,6,6,512]{3,2,1,0:T(8,128)(2,1)S(1)}, u32[]{:S(2)}, u32[]{:S(2)}) collective-permute-start(bf16[2,6,6,512]{3,2,1,0:T(8,128)(2,1)} %get-tuple-element.11), channel_id=1, source_target_pairs={{0,63},{1,32},{2,33},{3,34},{4,35},{5,36},{6,37},{7,38},{8,39},{9,... | collective-permute-start | bytes 221192 | tf_op jit(solution)/shard_map/ppermute | solution.py:361
  103.3 0.0 collective-permute-start.8
  103.3 0.6 fusion.1
  104.0 0.9 copy.15.up
  104.9 1.9 %copy.16.down = bf16[2,36,6,512]{3,2,1,0:T(8,128)(2,1)} copy(bf16[2,36,6,512]{3,0,2,1:T(2,128)(2,1)} %collective-permute-done.7) | data formatting | bytes 884736 | tf_op jit(solution)/shard_map/ppermute | solution.py:355
  106.8 4.8 %collective-permute-done.8.ul = bf16[2,6,6,512]{3,2,1,0:T(8,128)(2,1)S(1)} collective-permute-done((bf16[2,6,6,512]{3,2,1,0:T(8,128)(2,1)S(1)}, bf16[2,6,6,512]{3,2,1,0:T(8,128)(2,1)S(1)}, u32[]{:S(2)}, u32[]{:S(2)}) %collective-permute-start.8) | collective-permute-done | bytes 73760 | tf_op jit(solution)/shard_map/ppermute | solution.py:361
  111.7 0.6 copy-done.9
  112.2 0.3 copy-done
  112.5 0.2 copy-done.1
  112.7 70.3 %shard_map.119 = bf16[2,36,48,512]{3,2,1,0:T(8,128)(2,1)} custom-call(s32[2]{0:T(128)} %add_convert_fusion.flags, s32[14,1,288]{2,1,0:T(1,128)} %constant.14.clone.e_map, s32[14,1,288]{2,1,0:T(1,128)} %constant.15.clone.f_map, s32[48,64]{1,0:T(8,128)} %get-tuple-element.20.land, s32[48,64]{1,0:T(8,128)} %get-tuple-element.19.pad, ...), custom_call_target="tpu_custom_call" | custom-call | tf_op jit(solution)/shard_map/pallas_call | solution.py:326
  (26 shorter events, 0.1 us)
Async XLA Ops:
  0.0 19.8 %copy-start.2 = (s32[48,36]{0,1:T(8,128)S(1)}, s32[48,36]{0,1:T(8,128)}, u32[]{:S(2)}) copy-start(s32[48,36]{0,1:T(8,128)} %param.14) | copy-start | bytes 20740
  0.0 19.8 %copy-start.4 = (s32[48,36]{0,1:T(8,128)S(1)}, s32[48,36]{0,1:T(8,128)}, u32[]{:S(2)}) copy-start(s32[48,36]{0,1:T(8,128)} %param.13) | copy-start | bytes 20740
  0.9 18.9 %collective-permute-start = (s32[2,36,6]{2,1,0:T(8,128)S(1)}, s32[2,36,6]{2,1,0:T(8,128)S(1)}, u32[]{:S(2)}, u32[]{:S(2)}) collective-permute-start(s32[2,36,6]{2,1,0:T(8,128)S(1)} %get-tuple-element.21), channel_id=1, source_target_pairs={{0,32},{32,64},{64,96},{96,0},{1,33},{33,65},{65,97},{97,1},{2,34}... | collective-permute-start | bytes 5192 | tf_op jit(solution)/shard_map/ppermute | solution.py:355
  5.2 14.6 %collective-permute-start.1 = (s32[2,36,6]{2,1,0:T(8,128)S(1)}, s32[2,36,6]{2,1,0:T(8,128)S(1)}, u32[]{:S(2)}, u32[]{:S(2)}) collective-permute-start(s32[2,36,6]{2,1,0:T(8,128)S(1)} %get-tuple-element.22), channel_id=1, source_target_pairs={{0,96},{32,0},{64,32},{96,64},{1,97},{33,1},{65,33},{97,65},{2,98}... | collective-permute-start | bytes 5192 | tf_op jit(solution)/shard_map/ppermute | solution.py:355
  7.9 89.8 %collective-permute-start.6 = (bf16[2,36,6,512]{3,0,2,1:T(2,128)(2,1)}, bf16[2,36,6,512]{3,0,2,1:T(2,128)(2,1)S(1)}, u32[]{:S(2)}, u32[]{:S(2)}) collective-permute-start(bf16[2,36,6,512]{3,0,2,1:T(2,128)(2,1)} %copy.13), channel_id=1, source_target_pairs={{0,32},{32,64},{64,96},{96,0},{1,33},{33,65},{65,97},{97,1},{2,34}... | collective-permute-start | bytes 1327112 | tf_op jit(solution)/shard_map/ppermute | solution.py:355
  12.3 91.0 %collective-permute-start.7 = (bf16[2,36,6,512]{3,0,2,1:T(2,128)(2,1)}, bf16[2,36,6,512]{3,0,2,1:T(2,128)(2,1)}, u32[]{:S(2)}, u32[]{:S(2)}) collective-permute-start(bf16[2,36,6,512]{3,0,2,1:T(2,128)(2,1)} %copy.14), channel_id=1, source_target_pairs={{0,96},{32,0},{64,32},{96,64},{1,97},{33,1},{65,33},{97,65},{2,98}... | collective-permute-start | bytes 1327112 | tf_op jit(solution)/shard_map/ppermute | solution.py:355
  13.7 97.9 %collective-permute-start.5 = (bf16[2,6,48,512]{3,2,1,0:T(8,128)(2,1)S(1)}, bf16[2,6,48,512]{3,2,1,0:T(8,128)(2,1)S(1)}, u32[]{:S(2)}, u32[]{:S(2)}) collective-permute-start(bf16[2,6,48,512]{3,2,1,0:T(8,128)(2,1)S(1)} %get-tuple-element.15), channel_id=1, source_target_pairs={{0,31},{1,0},{2,1},{3,2},{4,3},{5,4},{6,5},{7,6},{8,7},{9,8},{10,9... | collective-permute-start | bytes 1769480 | tf_op jit(solution)/shard_map/ppermute | solution.py:355
  19.8 91.8 %collective-permute-start.4 = (bf16[2,6,48,512]{3,2,1,0:T(8,128)(2,1)S(1)}, bf16[2,6,48,512]{3,2,1,0:T(8,128)(2,1)S(1)}, u32[]{:S(2)}, u32[]{:S(2)}) collective-permute-start(bf16[2,6,48,512]{3,2,1,0:T(8,128)(2,1)S(1)} %get-tuple-element.16), channel_id=1, source_target_pairs={{0,1},{1,2},{2,3},{3,4},{4,5},{5,6},{6,7},{7,8},{8,9},{9,10},{10,1... | collective-permute-start | bytes 1769480 | tf_op jit(solution)/shard_map/ppermute | solution.py:355
  19.9 17.5 %collective-permute-start.2 = (s32[2,6,60]{2,1,0:T(8,128)S(1)}, s32[2,6,60]{2,1,0:T(8,128)S(1)}, u32[]{:S(2)}, u32[]{:S(2)}) collective-permute-start(s32[2,6,60]{2,1,0:T(8,128)S(1)} %get-tuple-element.17), channel_id=1, source_target_pairs={{0,1},{1,2},{2,3},{3,4},{4,5},{5,6},{6,7},{7,8},{8,9},{9,10},{10,1... | collective-permute-start | bytes 8648 | tf_op jit(solution)/shard_map/ppermute | solution.py:355
  37.4 50.9 %collective-permute-start.3 = (s32[2,6,60]{2,1,0:T(8,128)S(1)}, s32[2,6,60]{2,1,0:T(8,128)S(1)}, u32[]{:S(2)}, u32[]{:S(2)}) collective-permute-start(s32[2,6,60]{2,1,0:T(8,128)S(1)} %get-tuple-element.18), channel_id=1, source_target_pairs={{0,31},{1,0},{2,1},{3,2},{4,3},{5,4},{6,5},{7,6},{8,7},{9,8},{10,9... | collective-permute-start | bytes 8648 | tf_op jit(solution)/shard_map/ppermute | solution.py:355
  38.0 52.1 %copy-start.3 = (s32[48,36]{0,1:T(8,128)S(1)}, s32[48,36]{0,1:T(8,128)}, u32[]{:S(2)}) copy-start(s32[48,36]{0,1:T(8,128)} %param.14) | copy-start | bytes 20740
  38.0 52.1 %copy-start.5 = (s32[48,36]{0,1:T(8,128)S(1)}, s32[48,36]{0,1:T(8,128)}, u32[]{:S(2)}) copy-start(s32[48,36]{0,1:T(8,128)} %param.13) | copy-start | bytes 20740
  88.3 7.8 %collective-permute-start.11 = (bf16[2,6,6,512]{3,2,1,0:T(8,128)(2,1)S(1)}, bf16[2,6,6,512]{3,2,1,0:T(8,128)(2,1)S(1)}, u32[]{:S(2)}, u32[]{:S(2)}) collective-permute-start(bf16[2,6,6,512]{3,2,1,0:T(8,128)(2,1)S(1)} %get-tuple-element.9), channel_id=1, source_target_pairs={{0,127},{1,96},{2,97},{3,98},{4,99},{5,100},{6,101},{7,102},{8,103... | collective-permute-start | bytes 221192 | tf_op jit(solution)/shard_map/ppermute | solution.py:361
  96.2 15.5 %copy-start.6 = (bf16[2,6,6,512]{3,2,1,0:T(8,128)(2,1)}, bf16[2,6,6,512]{3,2,1,0:T(8,128)(2,1)S(1)}, u32[]{:S(2)}) copy-start(bf16[2,6,6,512]{3,2,1,0:T(8,128)(2,1)S(1)} %collective-permute-done.11.dr) | copy-start | bytes 221188
  96.2 10.6 %collective-permute-start.10 = (bf16[2,6,6,512]{3,2,1,0:T(8,128)(2,1)}, bf16[2,6,6,512]{3,2,1,0:T(8,128)(2,1)S(1)}, u32[]{:S(2)}, u32[]{:S(2)}) collective-permute-start(bf16[2,6,6,512]{3,2,1,0:T(8,128)(2,1)} %get-tuple-element.10), channel_id=1, source_target_pairs={{0,97},{1,98},{2,99},{3,100},{4,101},{5,102},{6,103},{7,104},{8,10... | collective-permute-start | bytes 221192 | tf_op jit(solution)/shard_map/ppermute | solution.py:361
  97.7 9.1 %collective-permute-start.9 = (bf16[2,6,6,512]{3,2,1,0:T(8,128)(2,1)}, bf16[2,6,6,512]{3,2,1,0:T(8,128)(2,1)S(1)}, u32[]{:S(2)}, u32[]{:S(2)}) collective-permute-start(bf16[2,6,6,512]{3,2,1,0:T(8,128)(2,1)} %get-tuple-element.11), channel_id=1, source_target_pairs={{0,63},{1,32},{2,33},{3,34},{4,35},{5,36},{6,37},{7,38},{8,39},{9,... | collective-permute-start | bytes 221192 | tf_op jit(solution)/shard_map/ppermute | solution.py:361
  103.3 8.3 %collective-permute-start.8 = (bf16[2,6,6,512]{3,2,1,0:T(8,128)(2,1)S(1)}, bf16[2,6,6,512]{3,2,1,0:T(8,128)(2,1)S(1)}, u32[]{:S(2)}, u32[]{:S(2)}) collective-permute-start(bf16[2,6,6,512]{3,2,1,0:T(8,128)(2,1)S(1)} %get-tuple-element.12), channel_id=1, source_target_pairs={{0,33},{1,34},{2,35},{3,36},{4,37},{5,38},{6,39},{7,40},{8,41},{9,... | collective-permute-start | bytes 221192 | tf_op jit(solution)/shard_map/ppermute | solution.py:361
  106.8 4.9 %copy-start.7 = (bf16[2,6,6,512]{3,2,1,0:T(8,128)(2,1)}, bf16[2,6,6,512]{3,2,1,0:T(8,128)(2,1)S(1)}, u32[]{:S(2)}) copy-start(bf16[2,6,6,512]{3,2,1,0:T(8,128)(2,1)S(1)} %collective-permute-done.10.dl) | copy-start | bytes 221188
  106.8 4.9 %copy-start.8 = (bf16[2,6,6,512]{3,2,1,0:T(8,128)(2,1)}, bf16[2,6,6,512]{3,2,1,0:T(8,128)(2,1)S(1)}, u32[]{:S(2)}) copy-start(bf16[2,6,6,512]{3,2,1,0:T(8,128)(2,1)S(1)} %collective-permute-done.9.ur) | copy-start | bytes 221188
  111.6 0.6 copy-start.9
  111.6 0.9 copy-start
  111.6 1.1 copy-start.1

commit v2 on v0

v2 whole, which is shorter than its diff:
```python
import functools
import math

import jax
import jax.numpy as jnp
import numpy as np
from jax import lax
from jax.experimental import pallas as pl
from jax.experimental.pallas import tpu as pltpu
from jax.sharding import PartitionSpec as P

F32, BF16 = jnp.float32, jnp.bfloat16
LOG2E = math.log2(math.e)
SCALE = LOG2E / math.sqrt(32.0)
W = 288
HALO = 576
PAY = HALO + 16
NEG = -1e30
MB = 1024 * 1024


def dot(a, b):
    return lax.dot_general(a, b, (((1,), (0,)), ((), ())), preferred_element_type=F32)


def dot_t(a, b):
    return lax.dot_general(a, b, (((1,), (1,)), ((), ())), preferred_element_type=F32)


def norm(x, g):
    c = x - jnp.mean(x, axis=-1, keepdims=True)
    s = jnp.mean(c * c, axis=-1, keepdims=True)
    return (c * lax.rsqrt(s + 1e-5) * g).astype(BF16)


def lanes(shape):
    return lax.broadcasted_iota(jnp.int32, shape, len(shape) - 1)


def rows(shape):
    return lax.broadcasted_iota(jnp.int32, shape, len(shape) - 2)


def gelu(x):
    return 0.5 * x * (1.0 + lax.erf(x * (1 / math.sqrt(2.0))))


def halves(cells):
    return cells[...].astype(F32).astype(BF16)


def attend_scratch(nq):
    return [
        pltpu.VMEM((8, 128), F32),
        pltpu.VMEM((2, 4, 4 * nq, 128), BF16),
        pltpu.VMEM((2, nq, 512), BF16),
        pltpu.VMEM((2, W, 512), BF16),
        pltpu.VMEM((2, 4, 1152, 128), BF16),
        pltpu.VMEM((2, 4 * nq, 128), BF16),
        pltpu.VMEM((2, W, 128), F32),
        pltpu.VMEM((2, nq, 256), F32),
        pltpu.VMEM((2, nq, 128), F32),
        pltpu.VMEM((1152, 128), BF16),
        *[pltpu.VMEM((4 * nq, 256), F32)] * 2,
        *[pltpu.VMEM((nq, 128), F32)] * 2,
        *[pltpu.VMEM((nq, 1152), BF16)] * 2,
    ]


def attend_setup(bias_ref, brow, ones):
    at = lanes((1, 128))
    for g in range(4):
        line = jnp.zeros((1, 128), F32)
        for h in range(4):
            full = jnp.full((1, 128), bias_ref[4 * g + h] * LOG2E, F32)
            hi = full.astype(BF16).astype(F32)
            mid = (full - hi).astype(BF16).astype(F32)
            for n, part in enumerate((hi, mid, full - hi - mid)):
                line = jnp.where(at == 3 * h + n, part, line)
        brow[g:g + 1] = line
    for h in range(4):
        hm = (at // 32 == h).astype(BF16)
        ones[256 * h:256 * h + 256] = jnp.broadcast_to(hm, (256, 128))
        ones[1024 + 32 * h:1056 + 32 * h] = jnp.broadcast_to(hm, (32, 128))


def pair(ws, own, tokens, land_row, blocked_row, gain, wqkv, out_row, ho, scratch):
    brow, qst, qpl, kpl, vst, lqx, lk, mk, mkt, ones, s0, s1, t0, t1, p0, p1 = scratch
    nq = qpl.shape[1]
    spot = lanes((1, 128))
    hms = [(spot // 32 == h).astype(BF16) for h in range(4)]
    threes = [(spot // 3 == h).astype(BF16) for h in range(4)]
    xn = jnp.concatenate([norm(tokens[w], gain) for w in ws], axis=0)
    xq = xn if nq == W else jnp.concatenate([xn[0:nq], xn[W:W + nq]], axis=0)
    for c in range(6):
        cols = slice(c * 256, (c + 1) * 256)
        if c < 2:
            r = (dot(xq, wqkv[:, cols]) * SCALE).astype(BF16)
            for a in range(2):
                ra = r[a * nq:(a + 1) * nq]
                qpl[a, :, cols] = ra
                for gl in range(2):
                    for h in range(4):
                        qst[a, 2 * c + gl, h * nq:(h + 1) * nq] = ra[:, gl * 128:(gl + 1) * 128] * hms[h]
        else:
            r = dot(xn, wqkv[:, cols]).astype(BF16)
            for a in range(2):
                ra = r[a * W:(a + 1) * W]
                if c < 4:
                    kpl[a, :, (c - 2) * 256:(c - 1) * 256] = ra
                    continue
                for gl in range(2):
                    g = 2 * (c - 4) + gl
                    for h in range(4):
                        vm = ra[:, gl * 128:(gl + 1) * 128] * hms[h]
                        vst[a, g, 256 * h:256 * h + 256] = vm[0:256]
                        vst[a, g, 1024 + 32 * h:1056 + 32 * h] = vm[256:288]
    eye = rows((W, W)) == lanes((W, W))
    for a, w in enumerate(ws):
        land = jnp.broadcast_to(jnp.sum(jnp.where(eye, land_row(w), 0.0), axis=1, keepdims=True), (W, 128))
        lk[a] = land
        lq = land[0:nq].astype(BF16)
        for h in range(4):
            lqx[a, h * nq:(h + 1) * nq] = lq * threes[h]
        mm = jnp.where(eye[0:nq], 0.0, blocked_row(w))
        mk[a] = mm[:, 0:256]
        mkt[a] = jnp.concatenate([mm[:, 256:288]] * 4, axis=1)

    ss, ts, ps = (s0, s1), (t0, t1), (p0, p1)

    def q_step(n):
        a, g, b = n // 4, n % 4, n % 2
        k = kpl[a, :, g * 128:(g + 1) * 128]
        kx = (lk[a] * brow[g:g + 1]).astype(BF16)
        ss[b][...] = dot_t(jnp.concatenate([qst[a, g], lqx[a]], axis=1), jnp.concatenate([k[0:256], kx[0:256]], axis=1))
        kt = jnp.concatenate([
            jnp.concatenate([k[256:288] * hms[h] for h in range(4)], axis=0),
            jnp.concatenate([kx[256:288] * threes[h] for h in range(4)], axis=0)], axis=1)
        lq = lk[a, 0:nq].astype(BF16)
        ts[b][...] = dot_t(jnp.concatenate([qpl[a, :, g * 128:(g + 1) * 128], lq], axis=1), kt)

    def s_step(n):
        a, b = n // 4, n % 2
        for r in range(0, own, 16):
            at = slice(r, min(r + 16, own))
            size = at.stop - r
            t = ts[b][at] + mkt[a, at]
            mask = mk[a, at]
            tops = []
            for h in range(4):
                s = ss[b][h * nq + r:h * nq + r + size] + mask
                m = jnp.maximum(jnp.maximum(s[:, :128], s[:, 128:]), jnp.where(spot // 32 == h, t, -3e38))
                m = jnp.max(m, axis=-1, keepdims=True)
                ps[b][at, h * 256:(h + 1) * 256] = jnp.exp2(s - m).astype(BF16)
                tops.append(m)
            top = jnp.where(spot < 32, tops[0], jnp.where(spot < 64, tops[1], jnp.where(spot < 96, tops[2], tops[3])))
            ps[b][at, 1024:1152] = jnp.exp2(t - top).astype(BF16)

    def v_step(n):
        a, g, b = n // 4, n % 4, n % 2
        o = dot(ps[b][0:own], jnp.concatenate([vst[a, g], ones[...]], axis=1))
        ho[pl.ds(out_row(ws[a]), own), g * 128:(g + 1) * 128] = (o[:, :128] / o[:, 128:]).astype(BF16)

    for n in range(10):
        if n < 8:
            q_step(n)
        if 1 <= n < 9:
            s_step(n - 1)
        if n >= 2:
            v_step(n - 2)


def feed_forward(res, gain, wup, wdown):
    xn = norm(res, gain)
    acc = res
    for c in range(4):
        hidden = gelu(dot(xn, wup[:, c * 512:(c + 1) * 512])).astype(BF16)
        acc = acc + dot(hidden, wdown[c * 512:(c + 1) * 512, :])
    return acc.astype(BF16)


def fetch(pairs, sems):
    copies = [pltpu.make_async_copy(src, dst, sems.at[n]) for n, (src, dst) in enumerate(pairs)]
    for c in copies:
        c.start()
    return copies


def pack_lon_body(first, last, land, pad, to_right, to_left):
    for strip, c0, to in ((last, 30, to_right), (first, 0, to_left)):
        to[0:HALO] = strip[...].reshape(HALO, 512)
        zero = jnp.zeros((10, 128), F32)
        a = jnp.concatenate([land[c0:c0 + 6].astype(F32), jnp.zeros((6, 80), F32)], axis=1)
        b = jnp.concatenate([pad[c0:c0 + 6].astype(F32), jnp.zeros((6, 80), F32)], axis=1)
        a = jnp.concatenate([a, zero], axis=0)
        b = jnp.concatenate([b, zero], axis=0)
        to[HALO:PAY] = jnp.concatenate([a, b, jnp.zeros((16, 256), F32)], axis=1).astype(BF16)


def wide_masks(land, pad, left, right, wide):
    l, r = left[HALO:PAY].astype(F32), right[HALO:PAY].astype(F32)
    for n, own in enumerate((land, pad)):
        wide[n, 0:6, 0:48] = l[0:6, 128 * n:128 * n + 48]
        wide[n, 6:42, 0:48] = own[...].astype(F32)
        wide[n, 42:48, 0:48] = r[0:6, 128 * n:128 * n + 48]


def pack_lat_body(x_low, x_high, left, right, land, pad, to_down, to_up, buf, wide):
    wide_masks(land, pad, left, right, wide)
    for to, xs, r0 in ((to_down, x_high, 42), (to_up, x_low, 0)):
        x0 = 10 if r0 else 0
        for l in range(2):
            for e in range(48):
                row = 6 * (48 * l + e)
                if e < 6 or e >= 42:
                    src, c = (left, e) if e < 6 else (right, e - 42)
                    a = (6 * l + c) * 48 + (32 if r0 else 0)
                    buf[row:row + 6] = src[a:a + 16].astype(F32)[x0:x0 + 6]
                else:
                    buf[row:row + 6] = xs[l, e - 6].astype(F32)[x0:x0 + 6]
        to[0:HALO] = buf[...].astype(BF16)
        pick = (lanes((16, 48)) == rows((16, 48)) + r0).astype(BF16)
        a = dot_t(pick, wide[0].astype(BF16)[:, 0:48])
        b = dot_t(pick, wide[1].astype(BF16)[:, 0:48])
        zero = jnp.zeros((16, 80), F32)
        tail = jnp.concatenate([a, zero, b, zero, jnp.zeros((16, 256), F32)], axis=1)
        to[HALO:PAY] = jnp.where(rows((16, 512)) < 6, tail, 0.0).astype(BF16)


def inner_attention_body(x, land, pad, g1, wqkv, bias, ho, xg, *scratch):
    attend_setup(bias, scratch[0], scratch[9])

    @pl.loop(0, 4)
    def _(n):
        l, jc = n // 2, n % 2
        for c in range(12):
            v = x[l, 6 + jc * 12 + c].astype(F32)
            for i in range(3):
                xg.at[jc * 3 + i, pl.ds(pl.multiple_of(l * 144, 8), 144), :][12 * c:12 * c + 12] = v[6 + 12 * i:18 + 12 * i]

    gain = g1[...]
    land_b, pad_b = halves(land), halves(pad)

    def row_of(cells, w):
        lane = lanes((1, W)) % 144
        here = rows((36, W)) == 6 + (w // 3) * 12 + lane // 12
        pick = (rows((48, W)) == 6 + (w % 3) * 12 + lane % 12).astype(BF16)
        return jnp.sum(jnp.where(here, dot(cells, pick), 0.0), axis=0, keepdims=True)

    @pl.loop(0, 3)
    def _(n):
        pair((2 * n, 2 * n + 1), W, xg, lambda w: row_of(land_b, w), lambda w: row_of(pad_b, w) * NEG, gain, wqkv,
             lambda w: pl.multiple_of(w * W, 32), ho, scratch)


def inner_rest_body(ho, x, wout, g2, wup_hbm, wdown_hbm, out, edge, att, nat, wup, wdown, sems):
    copies = fetch(((wup_hbm, wup), (wdown_hbm, wdown)), sems)

    @pl.loop(0, 2)
    def _(n):
        h = ho[pl.ds(pl.multiple_of(n * 3 * W, 32), 3 * W), :]
        for c in range(2):
            r = dot(h, wout[:, c * 256:(c + 1) * 256])
            for i in range(3):
                att[n * 3 + i, :, c * 256:(c + 1) * 256] = r[i * W:(i + 1) * W]

    @pl.loop(0, 4)
    def _(n):
        l, jc = n // 2, n % 2
        for c in range(12):
            k = n * 12 + c
            for i in range(3):
                nat[k, 6 + 12 * i:18 + 12 * i] = att.at[jc * 3 + i, pl.ds(pl.multiple_of(l * 144, 8), 144), :][12 * c:12 * c + 12]
            nat[k] = nat[k] + x[l, 6 + jc * 12 + c].astype(F32)
            edge[k, 0] = nat[k, 0:8]
            edge[k, 1] = nat[k, 40:48]

    for c in copies:
        c.wait()
    gain = g2[...]

    @pl.loop(0, 2)
    def _(n):
        res = nat[pl.ds(n * 24, 24), 8:40, :].reshape(768, 512)
        out[pl.ds(n * 24, 24)] = feed_forward(res, gain, wup, wdown).reshape(24, 32, 512)


def edge_windows():
    tens = [(i, j) for i in (1, 2, 3) for j in (0, 3)] + [(i, j) for i in (0, 4) for j in (1, 2)]
    return tens + [(i, j) for i in (0, 4) for j in (0, 3)]


def pieces(i, j):
    runs = {0: ((6, 6), (0, 6)), 4: ((48, 6), (54, 6))}.get(i, ((12 * i, 12),))
    cols = {0: (range(6, 12), range(0, 6)), 3: (range(36, 42), range(42, 48))}.get(j, (range(12 * j, 12 * j + 12),))
    return [(l, e, f, n) for es in cols for f, n in runs for l in range(2) for e in es]


def cell_maps():
    e_of, f_of = [], []
    for i, j in edge_windows():
        e_of.append([e for l, e, f, n in pieces(i, j) for _ in range(n)])
        f_of.append([f + a for l, e, f, n in pieces(i, j) for a in range(n)])
    return np.array(e_of, np.int32)[:, None], np.array(f_of, np.int32)[:, None]


def border_body(flags, e_map, f_map, land, pad, x, left, right, up, down, inner_hbm, edge, g1, wqkv, bias, wout_hbm, g2, wup_hbm, wdown_hbm,
                out, xg, ho, att, nat_s, nat_i, wide, inner, wout, wup, wdown, sems, *scratch):
    copies = fetch(((inner_hbm, inner), (wout_hbm, wout), (wup_hbm, wup), (wdown_hbm, wdown)), sems)
    attend_setup(bias, scratch[0], scratch[9])
    wide_masks(land, pad, left, right, wide)
    wins = edge_windows()

    for w, (i, j) in enumerate(wins):
        row = 0
        for l, e, f, n in pieces(i, j):
            if f < 6 or f >= 54:
                a = 6 * (48 * l + e)
                lo = a // 16 * 16
                seg = (up if f < 6 else down)[lo:lo + 32].astype(F32)[a - lo:a - lo + 6]
            elif 6 <= e < 42:
                seg = x[l, e - 6].astype(F32)[f - 6:f - 6 + n]
            else:
                src, c = (left, e) if e < 6 else (right, e - 42)
                a = (6 * l + c) * 48
                seg = src[a:a + 48].astype(F32)[f - 6:f - 6 + n]
            xg[w, row:row + n, :] = seg
            row += n

    gain1 = g1[...]
    masks = [wide[n].astype(BF16)[:, 0:48] for n in range(2)]
    beyond = [jnp.concatenate([up[HALO:PAY, 128 * n:128 * n + 48], down[HALO:PAY, 128 * n:128 * n + 48]], axis=0) for n in range(2)]

    def row_of(n, w):
        e, f = e_map[w], f_map[w]
        pick_f = (rows((48, W)) == f - 6).astype(BF16)
        pick_e = (rows((48, W)) == e).astype(BF16)
        far = jnp.where(f < 6, f, f - 54 + 16)
        far = jnp.where((f < 6) | (f >= 54), far, 99)
        mid = jnp.sum(jnp.where(rows((48, W)) == e, dot(masks[n], pick_f), 0.0), axis=0, keepdims=True)
        return mid + jnp.sum(jnp.where(rows((32, W)) == far, dot(beyond[n], pick_e), 0.0), axis=0, keepdims=True)

    def blocked(w):
        f = f_map[w]
        over = ((f < 6) & (flags[0] > 0)) | ((f >= 54) & (flags[1] > 0))
        return jnp.where(over | (row_of(1, w) > 0.5), NEG, 0.0)

    for own, first, last in ((144, 0, 5), (72, 5, 7)):
        @pl.loop(first, last)
        def _(n):
            pair((2 * n, 2 * n + 1), own, xg, lambda w: row_of(0, w), blocked, gain1, wqkv,
                 lambda w: pl.multiple_of(w * 144, 16), ho, scratch)

    for c in copies:
        c.wait()

    @pl.loop(0, 2)
    def _(n):
        h = ho[pl.ds(pl.multiple_of(n * 1008, 16), 1008), :]
        for c in range(2):
            a = dot(h, wout[:, c * 256:(c + 1) * 256])
            for i in range(7):
                att[7 * n + i, :, c * 256:(c + 1) * 256] = a[144 * i:144 * i + 144]

    side = {c: s for s, c in enumerate(list(range(6)) + list(range(30, 36)))}
    for w, (i, j) in enumerate(wins):
        row = 0
        for l, e, f, n in pieces(i, j):
            if row == (144 if w < 10 else 72):
                break
            c, r = e - 6, f - 6
            seg = att[w, row:row + n, :]
            if c in side:
                nat_s[l * 12 + side[c], r:r + n, :] = seg
            elif r == 0:
                nat_i[l * 24 + c - 6, 0, 0:6, :] = seg
            else:
                nat_i[l * 24 + c - 6, 1, 2:8, :] = seg
            row += n
    gain2 = g2[...]

    @pl.loop(0, 2)
    def _(l):
        xs = jnp.concatenate([x[l, 0:6], x[l, 30:36]], axis=0).astype(F32)
        res = nat_s[pl.ds(12 * l, 12)] + xs
        y = feed_forward(res.reshape(576, 512), gain2, wup, wdown).reshape(12, 48, 512)
        out[l, 0:6] = y[0:6]
        out[l, 30:36] = y[6:12]

    @pl.loop(0, 2)
    def _(l):
        xs = x[l, 6:30].astype(F32)
        at = nat_i[pl.ds(24 * l, 24)]
        ed = edge[pl.ds(24 * l, 24)]
        low = jnp.where(rows((1, 8, 512)) < 6, at[:, 0] + xs[:, 0:8], ed[:, 0])
        high = jnp.where(rows((1, 8, 512)) >= 2, at[:, 1] + xs[:, 40:48], ed[:, 1])
        res = jnp.concatenate([low.reshape(192, 512), high.reshape(192, 512)], axis=0)
        y = feed_forward(res, gain2, wup, wdown).astype(F32)
        full = jnp.concatenate([y[0:192].reshape(24, 8, 512), inner[pl.ds(24 * l, 24)].astype(F32), y[192:384].reshape(24, 8, 512)], axis=1)
        out[l, 6:30] = full.astype(BF16)


VM = pl.BlockSpec(memory_space=pltpu.VMEM)
SM = pl.BlockSpec(memory_space=pltpu.SMEM)
HBM = pl.BlockSpec(memory_space=pl.ANY)


def params():
    return pltpu.CompilerParams(vmem_limit_bytes=60 * MB)


def cost(flops, nbytes):
    return pl.CostEstimate(flops=flops, bytes_accessed=nbytes, transcendentals=0)


def pack_lon(xt, land, pad):
    strip = jax.ShapeDtypeStruct((PAY, 512), BF16)
    return pl.pallas_call(
        pack_lon_body, grid=(1,), out_shape=[strip] * 2,
        in_specs=[pl.BlockSpec((2, 6, 48, 512), lambda i: (0, 0, 0, 0)), pl.BlockSpec((2, 6, 48, 512), lambda i: (0, 5, 0, 0)), VM, VM],
        out_specs=[VM] * 2, compiler_params=pltpu.CompilerParams(vmem_limit_bytes=16 * MB), cost_estimate=cost(1, 2 * MB))(xt, xt, land, pad)


def pack_lat(xt, left, right, land, pad):
    strip = jax.ShapeDtypeStruct((PAY, 512), BF16)
    return pl.pallas_call(
        pack_lat_body, grid=(1,), out_shape=[strip] * 2,
        in_specs=[pl.BlockSpec((2, 36, 16, 512), lambda i: (0, 0, 0, 0)), pl.BlockSpec((2, 36, 16, 512), lambda i: (0, 0, 2, 0)), VM, VM, VM, VM],
        out_specs=[VM] * 2, scratch_shapes=[pltpu.VMEM((HALO, 512), F32), pltpu.VMEM((2, 48, 128), F32)],
        compiler_params=pltpu.CompilerParams(vmem_limit_bytes=24 * MB), cost_estimate=cost(1, 4 * MB))(xt, xt, left, right, land, pad)


def inner_attention(xt, land, pad, g1, wqkv, bias):
    return pl.pallas_call(
        inner_attention_body, out_shape=jax.ShapeDtypeStruct((6 * W, 512), BF16),
        in_specs=[VM] * 5 + [SM], out_specs=VM,
        scratch_shapes=[pltpu.VMEM((6, W, 512), F32)] + attend_scratch(W),
        compiler_params=params(), cost_estimate=cost(22 * 10**9, 8 * MB))(xt, land, pad, g1, wqkv, bias)


def inner_rest(ho, xt, wout, g2, wup, wdown):
    return pl.pallas_call(
        inner_rest_body, out_shape=[jax.ShapeDtypeStruct((48, 32, 512), BF16), jax.ShapeDtypeStruct((48, 2, 8, 512), F32)],
        in_specs=[VM] * 4 + [HBM] * 2, out_specs=[VM] * 2,
        scratch_shapes=[pltpu.VMEM((6, W, 512), F32), pltpu.VMEM((48, 48, 512), F32), pltpu.VMEM((512, 2048), BF16), pltpu.VMEM((2048, 512), BF16),
                        pltpu.SemaphoreType.DMA((2,))],
        compiler_params=params(), cost_estimate=cost(16 * 10**9, 10 * MB))(ho, xt, wout, g2, wup, wdown)


def border(flags, land, pad, xt, left, right, up, down, inner, edge, g1, wqkv, bias, wout, g2, wup, wdown):
    e_map, f_map = cell_maps()
    return pl.pallas_call(
        border_body, out_shape=jax.ShapeDtypeStruct((2, 36, 48, 512), BF16),
        in_specs=[SM] + [VM] * 9 + [HBM, VM, VM, VM, SM, HBM, VM, HBM, HBM], out_specs=VM,
        scratch_shapes=[
            pltpu.VMEM((14, W, 512), F32),
            pltpu.VMEM((14 * 144, 512), BF16),
            pltpu.VMEM((14, 144, 512), F32),
            pltpu.VMEM((24, 48, 512), F32),
            pltpu.VMEM((48, 2, 8, 512), F32),
            pltpu.VMEM((2, 48, 128), F32),
            pltpu.VMEM((48, 32, 512), BF16),
            pltpu.VMEM((512, 512), BF16),
            pltpu.VMEM((512, 2048), BF16),
            pltpu.VMEM((2048, 512), BF16),
            pltpu.SemaphoreType.DMA((4,)),
        ] + attend_scratch(144),
        compiler_params=params(), cost_estimate=cost(40 * 10**9, 20 * MB))(
            flags, jnp.asarray(e_map), jnp.asarray(f_map), land, pad, xt, left, right, up, down, inner, edge, g1, wqkv, bias, wout, g2, wup, wdown)


def from_behind(value, axis, by):
    devices = lax.axis_size(axis)
    return lax.ppermute(value, axis, [(i, (i + by) % devices) for i in range(devices)])


def on_device(latent_field, land_mask, padded, norm1_gain, qkv_weight, land_bias, out_weight, norm2_gain, up_weight, down_weight):
    xt = latent_field.transpose(0, 2, 1, 3)
    land, pad = land_mask.T, padded.T
    g1, g2 = norm1_gain.reshape(1, 512), norm2_gain.reshape(1, 512)
    lat = lax.axis_index("lat")
    flags = jnp.stack([(lat == 0).astype(jnp.int32), (lat == lax.axis_size("lat") - 1).astype(jnp.int32)])
    to_right, to_left = pack_lon(xt, land, pad)
    left, right = from_behind(to_right, "lon", 1), from_behind(to_left, "lon", -1)
    ho = inner_attention(xt, land, pad, g1, qkv_weight, land_bias)
    ho, left, right = lax.optimization_barrier((ho, left, right))
    to_down, to_up = pack_lat(xt, left, right, land, pad)
    up, down = from_behind(to_down, "lat", 1), from_behind(to_up, "lat", -1)
    inner, edge = inner_rest(ho, xt, out_weight, g2, up_weight, down_weight)
    y = border(flags, land, pad, xt, left, right, up, down, inner, edge, g1, qkv_weight, land_bias, out_weight, g2, up_weight, down_weight)
    return y.transpose(0, 2, 1, 3)


def solution(mesh):
    spec = P(None, "lat", "lon", None)
    placed = (spec, P("lat", "lon"), P("lat", "lon")) + (P(),) * 7
    return jax.shard_map(on_device, mesh=mesh, in_specs=placed, out_specs=spec, check_vma=False)
```

time: 375 us -> 104 us (0.28); the launches traced: 368 us -> 104 us
  matrix products: 208 us -> 0 us
  Pallas kernels: 0 us -> 85.5 us
  local copies, waits for them, and re-layouts: 70.9 us -> 5.76 us
  other arithmetic: 42.8 us -> 0.58 us
  waiting for transfers between devices: 30.4 us -> 0.68 us
    dot_general x14 -> x0, matrix products: 161 us -> none  [the longest x1 66.7 us: feed_forward(): jnp.dot(normed, up_weight, preferred_element_type=jnp.float32)]
    pallas_call x0 -> x5, Pallas kernels: none -> 85.5 us  [the longest x1 46 us: border(): pl.pallas_call(border_body, out_shape=jax.ShapeDtypeStruct((2, 36, 48, 51...]
    sub x4 -> x0, matrix products: 46.8 us -> none  [attend_windows(): raised = jnp.exp(scores - row_max)]
    ppermute x6 -> x4, waiting for transfers between devices: 30.4 us -> 0.68 us  [from_behind(): lax.ppermute(value, axis, [(i, (i + by) % devices) for i in range(devices)])]
    convert_element_type x5 -> x0, local copies, waits for them, and re-layouts: 22.6 us -> none  [the longest x4 18.7 us: attend_windows(): packed = jnp.einsum('wnd,de->wne', normed, qkv_weight, preferred_element_...]
    reduce_sum x10 -> x0, other arithmetic: 17.2 us -> none  [the longest x5 9.44 us: layer_norm(): spread = jnp.mean(center * center, axis=-1, keepdims=True)]
    reshape x4 -> x0, local copies, waits for them, and re-layouts: 15.4 us -> none  [the longest x1 8.9 us: feed_forward(): jnp.dot(hidden, down_weight, preferred_element_type=jnp.float32)]
    convert_element_type x7 -> x0, other arithmetic: 14 us -> none  [the longest x1 10.3 us: feed_forward(): return output.astype(jnp.bfloat16)]
  transfers between devices with their start and end apart: 6 -> 4, of which waited for: 3 -> 1; matrix products, arithmetic and copies ran while one was open for 5% -> 1% of each run, Pallas kernels for 0% -> 34%
where the time goes in v2:
time: 104 us
  Pallas kernels  85.5 us (82%)
  starting transfers between devices  11.3 us (11%)
  local copies, waits for them, and re-layouts  5.76 us (6%)
    pallas_call x1, Pallas kernels, border(): pl.pallas_call(border_body, out_shape=jax.ShapeDtypeStruct((2, 36, 48, 51...  46 us
    pallas_call x1, Pallas kernels, inner_attention(): pl.pallas_call(inner_attention_body, out_shape=jax.ShapeDtypeStruct((6 *...  21.8 us
    pallas_call x1, Pallas kernels, inner_rest(): pl.pallas_call(inner_rest_body, out_shape=[jax.ShapeDtypeStruct((48, 32,...  13.8 us
    ppermute x4, starting transfers between devices, from_behind(): lax.ppermute(value, axis, [(i, (i + by) % devices) for i in range(devices)])  11.3 us
    unnamed x16, local copies, waits for them, and re-layouts  5.76 us
    pallas_call x1, Pallas kernels, pack_lat(): pl.pallas_call(pack_lat_body, grid=(1,), out_shape=[strip] * 2, in_specs=...  2.79 us
  transfers between devices with their start and end apart: 4, of which 1 were waited for; matrix products, arithmetic and copies ran while one was open for 1% of the time, Pallas kernels for 34%

profile of v2, /device:TPU:1, one launch (start us, length us, event | category | flops | bytes accessed | tf_op | source)
XLA Modules:
  0.0 104.0 jit_solution(10936755714366710603)
XLA Ops:
  0.0 0.0 copy-start
  0.0 2.0 %copy-done = bf16[2,48,36,512]{3,1,2,0:T(8,128)(2,1)S(1)} copy-done((bf16[2,48,36,512]{3,1,2,0:T(8,128)(2,1)S(1)}, bf16[2,48,36,512]{3,1,2,0:T(8,128)(2,1)}, u32[]{:S(2)}) %copy-start) | copy-done | bytes 3538968
  2.0 0.0 copy-start.2
  2.0 0.7 copy-done.2
  2.7 0.0 copy-start.4
  2.7 0.7 copy-done.4
  3.5 1.1 %shard_map.119 = (bf16[592,512]{1,0:T(8,128)(2,1)}, bf16[592,512]{1,0:T(8,128)(2,1)}) custom-call(bf16[2,36,48,512]{3,2,1,0:T(8,128)(2,1)S(1)} %bitcast.11, bf16[2,36,48,512]{3,2,1,0:T(8,128)(2,1)S(1)} %bitcast.12, s32[36,48]{1,0:T(8,128)S(1)} %bitcast.17, s32[36,48]{1,0:T(8,128)S(1)} %bitcast.21), custom_call_target="tpu_custom_call" | custom-call | flops 1 | bytes 2097152 | tf_op jit(solution)/shard_map/pallas_call | solution.py:418
  4.6 2.5 %collective-permute-start = (bf16[592,512]{1,0:T(8,128)(2,1)}, bf16[592,512]{1,0:T(8,128)(2,1)}, u32[]{:S(2)}, u32[]{:S(2)}) collective-permute-start(bf16[592,512]{1,0:T(8,128)(2,1)} %get-tuple-element.14), channel_id=1, source_target_pairs={{0,1},{1,2},{2,3},{3,4},{4,5},{5,6},{6,7},{7,8},{8,9},{9,10},{10,1... | collective-permute-start | bytes 1818632 | tf_op jit(solution)/shard_map/ppermute | solution.py:474
  7.0 5.3 %collective-permute-start.1 = (bf16[592,512]{1,0:T(8,128)(2,1)}, bf16[592,512]{1,0:T(8,128)(2,1)}, u32[]{:S(2)}, u32[]{:S(2)}) collective-permute-start(bf16[592,512]{1,0:T(8,128)(2,1)} %get-tuple-element.15), channel_id=1, source_target_pairs={{0,31},{1,0},{2,1},{3,2},{4,3},{5,4},{6,5},{7,6},{8,7},{9,8},{10,9... | collective-permute-start | bytes 1818632 | tf_op jit(solution)/shard_map/ppermute | solution.py:474
  12.4 0.0 copy-start.1
  12.4 21.8 %shard_map.118.ho = bf16[1728,512]{1,0:T(8,128)(2,1)} custom-call(bf16[2,36,48,512]{3,2,1,0:T(8,128)(2,1)} %bitcast.8, s32[36,48]{1,0:T(8,128)} %bitcast.15, s32[36,48]{1,0:T(8,128)} %bitcast.19, f32[1,512]{1,0:T(1,128)} %bitcast.23, bf16[512,1536]{1,0:T(8,128)(2,1)} %wqkv.3, f32[16]{0:T(128)} %bias.3), custom_call_target="tpu_custom_call" | custom-call | flops 22000001024 | bytes 8388608 | tf_op jit(solution)/shard_map/pallas_call | solution.py:434
  34.2 0.6 add_convert_fusion.flags
  34.8 0.0 collective-permute-done.left
  34.8 0.0 collective-permute-done.1.right
  34.8 0.0 copy-done.1
  34.8 0.0 copy-start.3
  34.8 0.7 copy-done.3
  35.5 0.0 copy-start.5
  35.5 0.7 copy-done.5
  36.3 2.8 %shard_map.120 = (bf16[592,512]{1,0:T(8,128)(2,1)}, bf16[592,512]{1,0:T(8,128)(2,1)}) custom-call(bf16[2,36,48,512]{3,2,1,0:T(8,128)(2,1)S(1)} %bitcast.13, bf16[2,36,48,512]{3,2,1,0:T(8,128)(2,1)S(1)} %bitcast.14, bf16[592,512]{1,0:T(8,128)(2,1)} %collective-permute-done.left, bf16[592,512]{1,0:T(8,128)(2,1)} %collective-permute-done.1.right, ...), custom_call_target="tpu_custom_call" | custom-call | flops 1 | bytes 4194304 | tf_op jit(solution)/shard_map/pallas_call | solution.py:426
  39.0 3.5 %collective-permute-start.2 = (bf16[592,512]{1,0:T(8,128)(2,1)}, bf16[592,512]{1,0:T(8,128)(2,1)S(1)}, u32[]{:S(2)}, u32[]{:S(2)}) collective-permute-start(bf16[592,512]{1,0:T(8,128)(2,1)} %get-tuple-element.18), channel_id=1, source_target_pairs={{0,32},{32,64},{64,96},{96,0},{1,33},{33,65},{65,97},{97,1},{2,34}... | collective-permute-start | bytes 1818632 | tf_op jit(solution)/shard_map/ppermute | solution.py:474
  42.5 0.0 collective-permute-start.3
  42.5 13.8 %shard_map.121 = (bf16[48,32,512]{2,1,0:T(8,128)(2,1)}, f32[48,2,8,512]{3,2,1,0:T(8,128)}) custom-call(bf16[1728,512]{1,0:T(8,128)(2,1)} %shard_map.118.ho, bf16[2,36,48,512]{3,2,1,0:T(8,128)(2,1)} %bitcast.9, bf16[512,512]{1,0:T(8,128)(2,1)} %wout_hbm.1, f32[1,512]{1,0:T(1,128)} %bitcast.25, bf16[512,2048]{1,0:T(8,128)(2,1)} %wup_hbm.3, ...), custom_call_target="tpu_custom_call" | custom-call | flops 16000000000 | bytes 10485760 | tf_op jit(solution)/shard_map/pallas_call | solution.py:442
  56.3 0.0 collective-permute-done.2.up
  56.3 0.0 copy-start.6
  56.3 0.7 collective-permute-done.3.down
  57.0 0.0 copy-start.7
  57.0 0.2 copy-done.6
  57.2 0.7 copy-done.7
  57.9 46.0 %shard_map.122 = bf16[2,36,48,512]{3,2,1,0:T(8,128)(2,1)} custom-call(s32[2]{0:T(128)} %add_convert_fusion.flags, s32[14,1,288]{2,1,0:T(1,128)} %constant.14.clone.e_map, s32[14,1,288]{2,1,0:T(1,128)} %constant.15.clone.f_map, s32[36,48]{1,0:T(8,128)} %bitcast.16, s32[36,48]{1,0:T(8,128)} %bitcast.20, bf16[2,36,48,512]{3,2,1,0:T(8,128)(2,1)} %bitcast.10, ...), custom_call_target="tpu_custom_call" | custom-call | flops 40000000000 | bytes 20971520 | tf_op jit(solution)/shard_map/pallas_call | solution.py:452
Async XLA Ops:
  0.0 2.0 %copy-start = (bf16[2,48,36,512]{3,1,2,0:T(8,128)(2,1)S(1)}, bf16[2,48,36,512]{3,1,2,0:T(8,128)(2,1)}, u32[]{:S(2)}) copy-start(bf16[2,48,36,512]{3,1,2,0:T(8,128)(2,1)} %param.12) | copy-start | bytes 10616836
  2.0 0.7 copy-start.2
  2.7 0.7 copy-start.4
  4.6 30.2 %collective-permute-start = (bf16[592,512]{1,0:T(8,128)(2,1)}, bf16[592,512]{1,0:T(8,128)(2,1)}, u32[]{:S(2)}, u32[]{:S(2)}) collective-permute-start(bf16[592,512]{1,0:T(8,128)(2,1)} %get-tuple-element.14), channel_id=1, source_target_pairs={{0,1},{1,2},{2,3},{3,4},{4,5},{5,6},{6,7},{7,8},{8,9},{9,10},{10,1... | collective-permute-start | bytes 1818632 | tf_op jit(solution)/shard_map/ppermute | solution.py:474
  7.0 27.8 %collective-permute-start.1 = (bf16[592,512]{1,0:T(8,128)(2,1)}, bf16[592,512]{1,0:T(8,128)(2,1)}, u32[]{:S(2)}, u32[]{:S(2)}) collective-permute-start(bf16[592,512]{1,0:T(8,128)(2,1)} %get-tuple-element.15), channel_id=1, source_target_pairs={{0,31},{1,0},{2,1},{3,2},{4,3},{5,4},{6,5},{7,6},{8,7},{9,8},{10,9... | collective-permute-start | bytes 1818632 | tf_op jit(solution)/shard_map/ppermute | solution.py:474
  12.4 22.4 %copy-start.1 = (bf16[2,48,36,512]{3,1,2,0:T(8,128)(2,1)S(1)}, bf16[2,48,36,512]{3,1,2,0:T(8,128)(2,1)}, u32[]{:S(2)}) copy-start(bf16[2,48,36,512]{3,1,2,0:T(8,128)(2,1)} %param.12) | copy-start | bytes 10616836
  34.8 0.7 copy-start.3
  35.5 0.7 copy-start.5
  39.0 17.3 %collective-permute-start.2 = (bf16[592,512]{1,0:T(8,128)(2,1)}, bf16[592,512]{1,0:T(8,128)(2,1)S(1)}, u32[]{:S(2)}, u32[]{:S(2)}) collective-permute-start(bf16[592,512]{1,0:T(8,128)(2,1)} %get-tuple-element.18), channel_id=1, source_target_pairs={{0,32},{32,64},{64,96},{96,0},{1,33},{33,65},{65,97},{97,1},{2,34}... | collective-permute-start | bytes 1818632 | tf_op jit(solution)/shard_map/ppermute | solution.py:474
  42.5 14.5 %collective-permute-start.3 = (bf16[592,512]{1,0:T(8,128)(2,1)}, bf16[592,512]{1,0:T(8,128)(2,1)S(1)}, u32[]{:S(2)}, u32[]{:S(2)}) collective-permute-start(bf16[592,512]{1,0:T(8,128)(2,1)} %get-tuple-element.19), channel_id=1, source_target_pairs={{0,96},{32,0},{64,32},{96,64},{1,97},{33,1},{65,33},{97,65},{2,98}... | collective-permute-start | bytes 1818632 | tf_op jit(solution)/shard_map/ppermute | solution.py:474
  56.3 0.8 copy-start.6
  57.0 0.8 copy-start.7
